TPU v7x, 512 devices: a whole 4x8x8 slice. The times are simulated.
512 devices in a mesh: row: 16 (over x_lo, y), col: 32 (over x_hi, z, core).
Axes of the slice: x: 4 (x_hi: 2, x_lo: 2; x = x_hi * 2 + x_lo), y: 8, z: 8, core: 2. Of those that a mesh axis runs over, the one named last changes fastest.
Arguments:
- weight: bfloat16 [8192, 28672], P('row', 'col'), may hold values from -6 to 6
- eigenbasis: bfloat16 [28672, 28672], P('col', 'row'), may hold values from -0.03125 to 0.03125
- eigenvalues: float32 [28672], P('row'), may hold values from 0 to 10, as said below
- removed_local: int32 [32, 36], P('col'), may hold values from 0 to 895, as said below
- counts: int32 [32], replicated, may hold values from 1 to 36, 768 in all
Outputs:
- pruned: bfloat16 [8192, 28672], P('row', 'col')
Inputs may be any that keep to these rules, and one draw needn't show every extreme that they name: `removed_local`: row s holds distinct unit numbers of column shard s; its first counts[s] entries are that shard's removed units. The counts sum to 768; some shard removes exactly 36 units. `eigenvalues`: every entry is positive.
All inputs are finite; a program needn't handle non-finite values.
Results may differ from a plain program's by a relative error of at most 0.0075.
The roundings to bfloat16 on the way count: a program that leaves them out, or rounds other values in their place, can miss the bound.
Values may be sent and summed in bfloat16 or wider, within the bound.
A program may use at most 64 MiB of HBM per device.

v0:
```python
import jax
import jax.numpy as jnp
from jax import lax
from jax.sharding import Mesh
from jax.sharding import PartitionSpec as P

KDEV = 24
COL = ("col_0", "col_1", "col_2")
ROW = ("row_0", "row_1")


def laid_out(parts, dim):
    dims = list(parts.shape[1:])
    dims[dim] *= parts.shape[0]
    return jnp.moveaxis(parts, 0, dim).reshape(dims)


def gather_in_order(array, axes, sequence):
    parts = array
    for k in sequence:
        parts = lax.all_gather(parts, axes[k])
    done = sequence[::-1]
    back = [done.index(k) for k in range(len(axes))]
    parts = parts.transpose(*back, *range(len(axes), parts.ndim))
    return parts.reshape(-1, *array.shape)


def whole_of(array, axes, sequence, dim):
    return laid_out(gather_in_order(array, axes, sequence), dim)


def split_up(array, dim, count):
    before, after = (array.shape[:dim], array.shape[dim + 1 :])
    return jnp.moveaxis(array.reshape(*before, count, -1, *after), dim, 0)


def sum_at_owner(array, axis, dim):
    parts = split_up(array, dim, lax.axis_size(axis))
    arrived = lax.all_to_all(parts, axis, split_axis=0, concat_axis=0, tiled=True)
    return arrived.sum(axis=0)


def from_everyone(array, axis):
    count = lax.axis_size(axis)
    return lax.all_to_all(
        jnp.broadcast_to(array[None], (count, *array.shape)), axis, 0, 0, tiled=True
    )


def gathered_copies(array, axis, dim):
    parts = from_everyone(array, axis)
    return laid_out(parts, dim)


def compact_index(counts, removed_count, slot_count):
    shard_ends = jnp.cumsum(counts)
    shard_starts = shard_ends - counts
    positions = jnp.arange(removed_count, dtype=jnp.int32)
    owners = jnp.sum((shard_ends[None, :] <= positions[:, None]).astype(jnp.int32), axis=1)
    shard_ids = jnp.arange(counts.shape[0], dtype=jnp.int32)
    owner_start = jnp.sum(
        jnp.where(owners[:, None] == shard_ids[None, :], shard_starts[None, :], 0), axis=1
    )
    return owners * slot_count + positions - owner_start


def solve_rows(factor, weight_cols):
    targets = weight_cols.astype(jnp.float32).T
    forward = lax.linalg.triangular_solve(factor, targets, left_side=True, lower=True)
    backward = lax.linalg.triangular_solve(
        factor, forward, left_side=True, lower=True, transpose_a=True
    )
    return backward.T


def shards(weight, eigenbasis, eigenvalues, removed_local, counts):
    removed_count = KDEV * lax.axis_size(COL)
    slot_count = removed_local.shape[1]
    local_picks = removed_local[0]
    compact_order = compact_index(counts, removed_count, slot_count)
    chosen = jnp.take(eigenbasis, local_picks, axis=0).astype(jnp.float32)
    scaled = (chosen / eigenvalues[None, :]).astype(jnp.bfloat16)
    gathered = whole_of(scaled, COL, (0, 1, 2), 0)
    compacted = jnp.take(gathered, compact_order, axis=0)
    partial_value = lax.dot_general(
        compacted, eigenbasis, (((1,), (1,)), ((), ())), preferred_element_type=jnp.float32
    )
    share = sum_at_owner(partial_value, ROW, 0)
    block_share = jnp.take(share, local_picks, axis=1)
    block_band = lax.all_gather(block_share, COL, axis=1, tiled=True)
    block_whole = whole_of(block_band, ROW, (0, 1), 0)
    share_half = share.astype(jnp.bfloat16)
    block_matrix = jnp.take(block_whole, compact_order, axis=1)
    block_matrix = 0.5 * (block_matrix + block_matrix.T)
    factor = jnp.linalg.cholesky(block_matrix)
    weight_piece = jnp.take(weight, local_picks, axis=1)
    everything = gathered_copies(weight_piece, COL, 1)
    everything = jnp.take(everything, compact_order, axis=1)
    solved_half = solve_rows(factor, everything).astype(jnp.bfloat16)
    change = jnp.dot(
        solved_half,
        lax.all_gather(share_half, ROW, axis=0, tiled=True),
        preferred_element_type=jnp.float32,
    )
    return (weight.astype(jnp.float32) - change).astype(jnp.bfloat16)


def solution(mesh):
    torus = Mesh(mesh.devices.reshape(2, 8, 2, 8, 2), ("row_0", "row_1", "col_0", "col_1", "col_2"))
    return jax.shard_map(
        shards,
        mesh=torus,
        in_specs=(P(ROW, COL), P(COL, ROW), P(ROW), P(COL, None), P()),
        out_specs=P(ROW, COL),
        check_vma=False,
    )
```

profile of v0, /device:TPU:1, one launch (start us, length us, event | category | flops | bytes accessed | tf_op | source)
XLA Modules:
  0.0 566.5 jit_solution(6460981192097201665)
XLA Ops:
  9.9 6.8 %all_gather.34 = bf16[2,36,1792]{2,1,0:T(8,128)(2,1)} all-gather(bf16[1,36,1792]{2,1,0:T(8,128)(2,1)S(1)} %divide_convert_fusion), channel_id=1, replica_groups=mesh['row_0'=2,'row_1'=8,'col_0'=2,'col_1'=8,'col_2'=2] {'col_0'}, dimensions={0}, use_global_device_ids=true | all-gather | bytes 387072 | tf_op jit(solution)/shard_map/all_gather | solution.py:21
  16.8 48.2 %all-gather.12.cloned.1.call-done = bf16[16,36,1792]{2,1,0:T(8,128)(2,1)} async-done(((bf16[2,36,1792]{2,1,0:T(8,128)(2,1)}), bf16[16,36,1792]{2,1,0:T(8,128)(2,1)}) %all-gather.12.cloned.1.call-update) | async-done | bytes 2064400 | tf_op jit(solution)/shard_map/all_gather | solution.py:21
  65.0 4.6 copy.52
  70.2 24.1 %all-gather.14.cloned.1.call-done = bf16[16,2,36,1792]{3,1,0,2:T(2,128)(2,1)} async-done(((bf16[8,2,36,1792]{3,1,0,2:T(2,128)(2,1)}), bf16[16,2,36,1792]{3,1,0,2:T(2,128)(2,1)}) %all-gather.14.cloned.1.call-update) | async-done | bytes 4128784 | tf_op jit(solution)/shard_map/all_gather | solution.py:21
  96.9 3.4 copy.45
  100.3 6.9 %reshape_reshape.6 = bf16[1152,1792]{1,0:T(8,128)(2,1)} reshape(bf16[2,8,2,36,1792]{4,3,2,1,0:T(8,128)(2,1)} %copy.45) | data formatting | bytes 8257536 | tf_op jit(solution)/shard_map/reshape;reshape | solution.py:15
  107.3 9.1 %gather_fusion.1 = bf16[768,1792]{1,0:T(8,128)(2,1)} fusion(bf16[1152,1792]{1,0:T(8,128)(2,1)} %reshape_reshape.6, s32[1024]{0:T(1024)S(1)} %pad_clamp_fusion), kind=kCustom, calls=%fused_computation.1 | custom fusion | bytes 5508096 | tf_op jit(solution)/shard_map/jit(_take)/gather | solution.py:84
  116.4 4.8 fusion
  121.2 69.0 %all_to_all.10 = f32[16,48,896]{2,1,0:T(8,128)S(1)} all-to-all(f32[16,48,896]{2,1,0:T(8,128)S(1)} %bitcast.129), channel_id=1, replica_groups=mesh['row_0'=2,'row_1'=8,'col_0'=2,'col_1'=8,'col_2'=2] {'row_0','row_1'}, dimensions={0} | all-to-all | bytes 5505024 | tf_op jit(solution)/shard_map/all_to_all | solution.py:39
  191.2 46.8 %all-gather.4 = f32[32,36,48]{2,1,0:T(8,128)S(1)} all-gather(f32[1,36,48]{2,1,0:T(8,128)S(1)} %select_bitcast_fusion.7), channel_id=1, replica_groups=mesh['row_0'=2,'row_1'=8,'col_0'=2,'col_1'=8,'col_2'=2] {'col_0','col_1'..., dimensions={0}, use_global_device_ids=true | all-gather | bytes 228096 | tf_op jit(solution)/shard_map/all_gather | solution.py:90
  238.3 7.7 %all-gather.2 = f32[96,1152]{1,0:T(8,128)} all-gather(f32[48,1152]{1,0:T(8,128)S(1)} %bitcast.132), channel_id=4, replica_groups=mesh['row_0'=2,'row_1'=8,'col_0'=2,'col_1'=8,'col_2'=2] {'row_0'}, dimensions={0}, use_global_device_ids=true | all-gather | bytes 663552 | tf_op jit(solution)/shard_map/all_gather | solution.py:21
  248.4 4.6 all-to-all-start.1
  253.0 10.9 %all-gather.10.cloned.1.call-start = ((), (), s32[]{:S(2)}) async-start(), calls=%async_computation.2 | async-start | bytes 1462272 | tf_op jit(solution)/shard_map/all_gather | solution.py:102
  263.9 23.4 %all-to-all-done.1 = bf16[32,512,36]{1,2,0:T(8,128)(2,1)S(1)} async-done(((bf16[32,512,36]{1,2,0:T(8,128)(2,1)}), bf16[32,512,36]{1,2,0:T(8,128)(2,1)S(1)}, u32[]{:S(2)}, u32[]{:S(2)}) %all-to-all-start.1) | async-done | bytes 1179680 | tf_op jit(solution)/shard_map/all_to_all | solution.py:45
  292.6 4.0 copy.48
  296.7 5.2 copy.49
  301.8 5.5 gather_fusion.3
  309.0 3.0 copy.50
  315.5 11.7 %cholesky.164 = f32[128,128]{1,0:T(8,128)S(1)} custom-call(f32[128,128]{1,0:T(8,128)S(1)} %cholesky.421), custom_call_target="Cholesky" | custom-call | tf_op jit(solution)/shard_map/jit(cholesky)/cholesky | solution.py:95
  327.4 9.8 %custom-call.48 = f32[1,128,128]{1,2,0:T(8,128)S(1)} custom-call(f32[1,128,128]{2,1,0:T(8,128)S(1)} %get-tuple-element.40), custom_call_target="InvertDiagBlocksLowerTriangular" | custom-call | tf_op jit(solution)/shard_map/jit(cholesky)/cholesky | solution.py:95
  340.0 11.7 %cholesky.187 = f32[128,128]{1,0:T(8,128)S(1)} custom-call(f32[128,128]{1,0:T(8,128)S(1)} %cholesky.425), custom_call_target="Cholesky" | custom-call | tf_op jit(solution)/shard_map/jit(cholesky)/cholesky | solution.py:95
  351.8 10.2 %custom-call.49 = f32[1,128,128]{1,2,0:T(8,128)S(1)} custom-call(f32[1,128,128]{2,1,0:T(8,128)S(1)} %get-tuple-element.37), custom_call_target="InvertDiagBlocksLowerTriangular" | custom-call | tf_op jit(solution)/shard_map/jit(cholesky)/cholesky | solution.py:95
  363.9 11.7 %cholesky.352 = f32[128,128]{1,0:T(8,128)S(1)} custom-call(f32[128,128]{1,0:T(8,128)S(1)} %cholesky.430), custom_call_target="Cholesky" | custom-call | tf_op jit(solution)/shard_map/jit(cholesky)/cholesky | solution.py:95
  376.3 9.8 %custom-call.50 = f32[1,128,128]{1,2,0:T(8,128)S(1)} custom-call(f32[1,128,128]{2,1,0:T(8,128)S(1)} %get-tuple-element.34), custom_call_target="InvertDiagBlocksLowerTriangular" | custom-call | tf_op jit(solution)/shard_map/jit(cholesky)/cholesky | solution.py:95
  388.0 11.9 %cholesky.371 = f32[128,128]{1,0:T(8,128)S(1)} custom-call(f32[128,128]{1,0:T(8,128)S(1)} %cholesky.435), custom_call_target="Cholesky" | custom-call | tf_op jit(solution)/shard_map/jit(cholesky)/cholesky | solution.py:95
  400.5 9.8 %custom-call.51 = f32[1,128,128]{1,2,0:T(8,128)S(1)} custom-call(f32[1,128,128]{2,1,0:T(8,128)S(1)} %get-tuple-element.31), custom_call_target="InvertDiagBlocksLowerTriangular" | custom-call | tf_op jit(solution)/shard_map/jit(cholesky)/cholesky | solution.py:95
  412.1 11.7 %cholesky.390 = f32[128,128]{1,0:T(8,128)S(1)} custom-call(f32[128,128]{1,0:T(8,128)S(1)} %cholesky.440), custom_call_target="Cholesky" | custom-call | tf_op jit(solution)/shard_map/jit(cholesky)/cholesky | solution.py:95
  424.6 9.8 %custom-call.52 = f32[1,128,128]{1,2,0:T(8,128)S(1)} custom-call(f32[1,128,128]{2,1,0:T(8,128)S(1)} %get-tuple-element.28), custom_call_target="InvertDiagBlocksLowerTriangular" | custom-call | tf_op jit(solution)/shard_map/jit(cholesky)/cholesky | solution.py:95
  435.9 11.9 %cholesky.408 = f32[128,128]{1,0:T(8,128)S(1)} custom-call(f32[128,128]{1,0:T(8,128)S(1)} %convolution_subtract_fusion.14), custom_call_target="Cholesky" | custom-call | tf_op jit(solution)/shard_map/jit(cholesky)/cholesky | solution.py:95
  454.6 20.3 %while.1 = (s32[]{:T(128)}, f32[768,768]{1,0:T(8,128)}, s32[6,2]{0,1:T(2,128)S(1)}, f32[6,128,128]{2,1,0:T(8,128)}, s32[]{:T(128)}) while((s32[]{:T(128)}, f32[768,768]{1,0:T(8,128)}, s32[6,2]{0,1:T(2,128)S(1)}, f32[6,128,128]{2,1,0:T(8,128)}, s32[]{:T(128)}) %tuple.39), condition=%wide.while_cond, body=%wide.while_body.sunk | while | flops 2 | bytes 132705 | solution.py:70
  475.0 60.5 %custom-call.53 = f32[6,128,128]{1,2,0:T(8,128)} custom-call(f32[6,128,128]{2,1,0:T(8,128)} %get-tuple-element.12), custom_call_target="InvertDiagBlocksLowerTriangular" | custom-call | tf_op jit(solution)/shard_map/triangular_solve | solution.py:70
  555.4 4.1 subtract_convert_fusion
  (137 shorter events, 75.9 us)
Async XLA Ops:
  6.5 1.9 copy-start
  6.5 58.5 %all-gather.12.cloned.1.call-start = ((), (), s32[]{:S(2)}) async-start(), calls=%async_computation.3 | async-start | bytes 2580480 | tf_op jit(solution)/shard_map/all_gather | solution.py:21
  16.8 77.5 %all-gather.14.cloned.1.call-start = ((), (), s32[]{:S(2)}) async-start(), calls=%async_computation.4 | async-start | bytes 6193152 | tf_op jit(solution)/shard_map/all_gather | solution.py:21
  65.0 4.7 copy-start.7
  69.6 223.0 %all-gather.16.cloned.1.call-start = ((), (), s32[]{:S(2)}) async-start(), calls=%async_computation.5 | async-start | bytes 3981312 | tf_op jit(solution)/shard_map/all_gather | solution.py:21
  190.4 55.6 %copy-start.6 = (bf16[512,896]{1,0:T(8,128)(2,1)S(1)}, bf16[512,896]{1,0:T(8,128)(2,1)}, u32[]{:S(2)}) copy-start(bf16[512,896]{1,0:T(8,128)(2,1)} %param.5) | copy-start | bytes 2752516
  248.4 38.9 %all-to-all-start.1 = ((bf16[32,512,36]{1,2,0:T(8,128)(2,1)}), bf16[32,512,36]{1,2,0:T(8,128)(2,1)S(1)}, u32[]{:S(2)}, u32[]{:S(2)}) async-start(bf16[32,512,36]{1,2,0:T(8,128)(2,1)} %broadcast_in_dim.99), calls=%async_computation.1 | async-start | bytes 2621440 | tf_op jit(solution)/shard_map/all_to_all | solution.py:45
  253.0 302.5 %all-gather.10.cloned.1.call-start = ((), (), s32[]{:S(2)}) async-start(), calls=%async_computation.2 | async-start | bytes 1462272 | tf_op jit(solution)/shard_map/all_gather | solution.py:102
  314.1 1.4 copy-start.3
  475.0 64.6 %copy-start.2 = (f32[768,768]{1,0:T(8,128)S(1)}, f32[768,768]{1,0:T(8,128)}, u32[]{:S(2)}) copy-start(f32[768,768]{1,0:T(8,128)} %get-tuple-element.109) | copy-start | bytes 7077892
  535.5 6.7 %copy-start.4 = (f32[768,512]{1,0:T(8,128)S(1)}, f32[768,512]{1,0:T(8,128)}, u32[]{:S(2)}) copy-start(f32[768,512]{1,0:T(8,128)} %get-tuple-element.21) | copy-start | bytes 4718596
  538.2 4.6 copy-start.5
  554.8 4.8 copy-start.1
Sparse Core Ops, SparseCore 0:
  16.9 48.0 all-gather.11
  69.7 24.4 all-gather.13
  246.1 41.4 all-gather.15
  292.7 59.1 all-gather.9
where the time goes:
time: 576 us; the launch traced here: 566 us
  other arithmetic  198 us (34%)
  blocking collectives  130 us (23%)
  waiting for transfers between devices  95.8 us (17%)
  local copies, waits for them, and re-layouts  74.4 us (13%)
  matrix products  35 us (6%)
  between operations  17.8 us (3%)
  starting transfers between devices  15.5 us (3%)
    another operation x22, other arithmetic, shards(): factor = jnp.linalg.cholesky(block_matrix)  124 us
    all_gather x3, waiting for transfers between devices, gather_in_order(): parts = lax.all_gather(parts, axes[k])  72.3 us
    all_to_all x1, blocking collectives, sum_at_owner(): lax.all_to_all(parts, axis, split_axis=0, concat_axis=0, tiled=True)  69 us
    another operation x4, other arithmetic, solve_rows(): lax.linalg.triangular_solve(factor, forward, left_side=True, lower=True,...  62.8 us
    all_gather x1, blocking collectives, shards(): block_band = lax.all_gather(block_share, COL, axis=1, tiled=True)  46.8 us
    all_to_all x1, waiting for transfers between devices, from_everyone(): lax.all_to_all(jnp.broadcast_to(array[None], (count, *array.shape)), axis...  23.4 us
    another operation x19, local copies, waits for them, and re-layouts  20.4 us
    all_gather x2, blocking collectives, gather_in_order(): parts = lax.all_gather(parts, axes[k])  14.5 us
  transfers between devices with their start and end apart: 5, of which 3 were waited for; matrix products, arithmetic and copies ran while one was open for 47% of the time, Pallas kernels for 0%

commit v1 on v0

--- a/solution.py
+++ b/solution.py
@@ -1,6 +1,9 @@
+import functools
 import jax
 import jax.numpy as jnp
 from jax import lax
+from jax.experimental import pallas as pl
+from jax.experimental.pallas import tpu as pltpu
 from jax.sharding import Mesh
 from jax.sharding import PartitionSpec as P
 
@@ -53,24 +56,91 @@
 
 
 def compact_index(counts, removed_count, slot_count):
-    shard_ends = jnp.cumsum(counts)
-    shard_starts = shard_ends - counts
+    shard_ids = jnp.arange(counts.shape[0], dtype=jnp.int32)
+    shard_starts = jnp.sum(jnp.where(shard_ids[None, :] < shard_ids[:, None], counts[None, :], 0), axis=1)
+    shard_ends = shard_starts + counts
     positions = jnp.arange(removed_count, dtype=jnp.int32)
     owners = jnp.sum((shard_ends[None, :] <= positions[:, None]).astype(jnp.int32), axis=1)
-    shard_ids = jnp.arange(counts.shape[0], dtype=jnp.int32)
     owner_start = jnp.sum(
         jnp.where(owners[:, None] == shard_ids[None, :], shard_starts[None, :], 0), axis=1
     )
     return owners * slot_count + positions - owner_start
 
 
-def solve_rows(factor, weight_cols):
-    targets = weight_cols.astype(jnp.float32).T
-    forward = lax.linalg.triangular_solve(factor, targets, left_side=True, lower=True)
-    backward = lax.linalg.triangular_solve(
-        factor, forward, left_side=True, lower=True, transpose_a=True
-    )
-    return backward.T
+HI = lax.Precision.HIGHEST
+NB=128
+
+def invert_block(block):
+    lane = lax.broadcasted_iota(jnp.int32, (8, NB), 1)
+    sub = lax.broadcasted_iota(jnp.int32, (8, NB), 0)
+    tiles = [block[8 * i : 8 * i + 8, :] for i in range(NB // 8)]
+    for b in range(NB // 8):
+        here = (lane >= 8 * b) & (lane < 8 * b + 8)
+        columns = [[jnp.broadcast_to(t[:, 8 * b + j : 8 * b + j + 1], (8, NB)) for j in range(8)] for t in tiles]
+        pivots = list(columns[b])
+        panel = jnp.where(here, jnp.where(lane - 8 * b == sub, 1.0, 0.0), tiles[b])
+        for p in range(8):
+            own = sub == p
+            factor = pivots[p]
+            inv = 1.0 / jnp.broadcast_to(factor[p : p + 1, :], (8, NB))
+            def step(x):
+                scaled = jnp.broadcast_to(x[p : p + 1, :], (8, NB)) * inv
+                return jnp.where(own, scaled, x - factor * scaled)
+            for q in range(p + 1, 8):
+                pivots[q] = step(pivots[q])
+            panel = step(panel)
+        rows = [jnp.broadcast_to(panel[j : j + 1, :], (8, NB)) for j in range(8)]
+        for i in range(NB // 8):
+            if i == b:
+                tiles[i] = panel
+            else:
+                t = jnp.where(here, 0.0, tiles[i])
+                parts = [columns[i][j] * rows[j] for j in range(8)]
+                while len(parts) > 1:
+                    parts = [parts[2 * m] + parts[2 * m + 1] for m in range(len(parts) // 2)]
+                tiles[i] = t - parts[0]
+    return jnp.concatenate(tiles, axis=0)
+
+def solve_kernel(nblk, matrix_ref, target_ref, out_ref, aug, upper, sol):
+    width = nblk * NB
+    for i in range(nblk):
+        aug[i, :, :width] = matrix_ref[i * NB : (i + 1) * NB, :]
+        aug[i, :, width:] = target_ref[i * NB : (i + 1) * NB, :].astype(jnp.float32)
+
+    def eliminate(k, _):
+        here = pl.ds(pl.multiple_of(k * NB, NB), NB)
+        inverse = invert_block(aug[k, :, here])
+        panel = jnp.dot(inverse, aug[k], preferred_element_type=jnp.float32, precision=HI)
+        upper[k] = panel
+
+        def update(i, _):
+            there = pl.ds(pl.multiple_of(i * NB, NB), NB)
+            aug[i] -= lax.dot_general(aug[k, :, there], upper[k], (((0,), (0,)), ((), ())),
+                                      preferred_element_type=jnp.float32, precision=HI)
+            return 0
+        lax.fori_loop(k + 1, nblk, update, 0)
+        return 0
+    lax.fori_loop(0, nblk, eliminate, 0)
+    for k in range(nblk - 1, -1, -1):
+        x = upper[k, :, width:]
+        if k < nblk - 1:
+            x = x - jnp.dot(upper[k, :, (k + 1) * NB : width], sol[(k + 1) * NB :, :],
+                            preferred_element_type=jnp.float32, precision=HI)
+        sol[k * NB : (k + 1) * NB, :] = x
+        out_ref[k * NB : (k + 1) * NB, :] = x.astype(jnp.bfloat16)
+
+def solve(matrix, targets):
+    k, d = targets.shape
+    nblk = k // NB
+    return pl.pallas_call(
+        functools.partial(solve_kernel, nblk),
+        out_shape=jax.ShapeDtypeStruct((k, d), jnp.bfloat16),
+        in_specs=[pl.BlockSpec(memory_space=pltpu.VMEM)] * 2,
+        out_specs=pl.BlockSpec(memory_space=pltpu.VMEM),
+        scratch_shapes=[pltpu.VMEM((nblk, NB, k + d), jnp.float32), pltpu.VMEM((nblk, NB, k + d), jnp.float32),
+                        pltpu.VMEM((k, d), jnp.float32)],
+        compiler_params=pltpu.CompilerParams(vmem_limit_bytes=40 << 20),
+    )(matrix, targets)
 
 
 def shards(weight, eigenbasis, eigenvalues, removed_local, counts):
@@ -92,14 +162,14 @@
     share_half = share.astype(jnp.bfloat16)
     block_matrix = jnp.take(block_whole, compact_order, axis=1)
     block_matrix = 0.5 * (block_matrix + block_matrix.T)
-    factor = jnp.linalg.cholesky(block_matrix)
     weight_piece = jnp.take(weight, local_picks, axis=1)
     everything = gathered_copies(weight_piece, COL, 1)
     everything = jnp.take(everything, compact_order, axis=1)
-    solved_half = solve_rows(factor, everything).astype(jnp.bfloat16)
-    change = jnp.dot(
+    solved_half = solve(block_matrix, everything.T)
+    change = lax.dot_general(
         solved_half,
         lax.all_gather(share_half, ROW, axis=0, tiled=True),
+        (((0,), (0,)), ((), ())),
         preferred_element_type=jnp.float32,
     )
     return (weight.astype(jnp.float32) - change).astype(jnp.bfloat16)

time: 576 us -> 403 us (0.70)
  the two profiles are of different devices: /device:TPU:1 before, /device:TPU:64 now
where the time goes in v1:
time: 403 us; the launch traced here: 402 us
  blocking collectives  132 us (33%)
  waiting for transfers between devices  104 us (26%)
  local copies, waits for them, and re-layouts  66.5 us (17%)
  Pallas kernels  54.6 us (14%)
  other arithmetic  13.8 us (3%)
  between operations  13.2 us (3%)
  starting transfers between devices  8.93 us (2%)
  matrix products  8.59 us (2%)
    all_to_all x1, blocking collectives, sum_at_owner(): lax.all_to_all(parts, axis, split_axis=0, concat_axis=0, tiled=True)  72.7 us
    all_gather x3, waiting for transfers between devices, gather_in_order(): parts = lax.all_gather(parts, axes[k])  68.4 us
    pallas_call x1, Pallas kernels, solve(): pl.pallas_call(functools.partial(solve_kernel, nblk), out_shape=jax.Shape...  54.6 us
    all_gather x1, blocking collectives, shards(): block_band = lax.all_gather(block_share, COL, axis=1, tiled=True)  42.9 us
    all_to_all x1, waiting for transfers between devices, from_everyone(): lax.all_to_all(jnp.broadcast_to(array[None], (count, *array.shape)), axis...  35.4 us
    all_gather x2, blocking collectives, gather_in_order(): parts = lax.all_gather(parts, axes[k])  16.8 us
    another operation x2, local copies, waits for them, and re-layouts, laid_out(): return jnp.moveaxis(parts, 0, dim).reshape(dims)  12.1 us
    gather x1, local copies, waits for them, and re-layouts, shards(): compacted = jnp.take(gathered, compact_order, axis=0)  9.11 us
  transfers between devices with their start and end apart: 5, of which 3 were waited for; matrix products, arithmetic and copies ran while one was open for 10% of the time, Pallas kernels for 14%

profile of v1, /device:TPU:64, one launch (start us, length us, event | category | flops | bytes accessed | tf_op | source)
XLA Modules:
  0.0 401.9 jit_solution(4852548267431030923)
XLA Ops:
  9.9 7.8 %all_gather.34 = bf16[2,36,1792]{2,1,0:T(8,128)(2,1)} all-gather(bf16[1,36,1792]{2,1,0:T(8,128)(2,1)S(1)} %divide_convert_fusion), channel_id=1, replica_groups=mesh['row_0'=2,'row_1'=8,'col_0'=2,'col_1'=8,'col_2'=2] {'col_0'}, dimensions={0}, use_global_device_ids=true | all-gather | bytes 387072 | tf_op jit(solution)/shard_map/all_gather | solution.py:24
  17.8 48.3 %all-gather.12.cloned.1.call-done = bf16[16,36,1792]{2,1,0:T(8,128)(2,1)} async-done(((bf16[2,36,1792]{2,1,0:T(8,128)(2,1)}), bf16[16,36,1792]{2,1,0:T(8,128)(2,1)}) %all-gather.12.cloned.1.call-update) | async-done | bytes 2064400 | tf_op jit(solution)/shard_map/all_gather | solution.py:24
  66.1 4.6 %copy.46 = bf16[8,2,36,1792]{3,1,0,2:T(2,128)(2,1)} copy(bf16[8,2,36,1792]{3,2,1,0:T(8,128)(2,1)} %bitcast.39) | data formatting | bytes 4128768 | tf_op jit(solution)/shard_map/all_gather | solution.py:24
  71.2 20.1 %all-gather.14.cloned.1.call-done = bf16[16,2,36,1792]{3,1,0,2:T(2,128)(2,1)} async-done(((bf16[8,2,36,1792]{3,1,0,2:T(2,128)(2,1)}), bf16[16,2,36,1792]{3,1,0,2:T(2,128)(2,1)}) %all-gather.14.cloned.1.call-update) | async-done | bytes 4128784 | tf_op jit(solution)/shard_map/all_gather | solution.py:24
  91.2 2.7 copy.49
  93.9 3.4 copy.39
  97.3 7.0 %reshape_reshape.6 = bf16[1152,1792]{1,0:T(8,128)(2,1)} reshape(bf16[2,8,2,36,1792]{4,3,2,1,0:T(8,128)(2,1)} %copy.39) | data formatting | bytes 8257536 | tf_op jit(solution)/shard_map/reshape;reshape | solution.py:18
  104.3 9.1 %gather_fusion.1 = bf16[768,1792]{1,0:T(8,128)(2,1)} fusion(bf16[1152,1792]{1,0:T(8,128)(2,1)} %reshape_reshape.6, s32[1024]{0:T(1024)S(1)} %pad_clamp_fusion), kind=kCustom, calls=%fused_computation.1 | custom fusion | bytes 5508096 | tf_op jit(solution)/shard_map/jit(_take)/gather | solution.py:154
  113.4 4.8 %fusion = f32[768,896]{1,0:T(8,128)S(1)} fusion(bf16[896,1792]{1,0:T(8,128)(2,1)S(1)} %copy-done, bf16[768,1792]{1,0:T(8,128)(2,1)} %gather_fusion.1, pred[768]{0:T(1024)(128)(4,1)S(1)} %compare_and_fusion), kind=kOutput, calls=%fused_computation.7 | convolution fusion | flops 2467627008 | bytes 8717056 | tf_op jit(solution)/shard_map/dot_general | solution.py:155
  118.2 72.7 %all_to_all.10 = f32[16,48,896]{2,1,0:T(8,128)} all-to-all(f32[16,48,896]{2,1,0:T(8,128)S(1)} %bitcast.38), channel_id=1, replica_groups=mesh['row_0'=2,'row_1'=8,'col_0'=2,'col_1'=8,'col_2'=2] {'row_0','row_1'}, dimensions={0} | all-to-all | bytes 5505024 | tf_op jit(solution)/shard_map/all_to_all | solution.py:42
  190.9 1.9 reduce_sum.42
  193.8 1.6 gather_fusion.2
  195.5 42.9 %all-gather.4 = f32[32,36,48]{2,1,0:T(8,128)} all-gather(f32[1,36,48]{2,1,0:T(8,128)S(1)} %select_bitcast_fusion.2), channel_id=1, replica_groups=mesh['row_0'=2,'row_1'=8,'col_0'=2,'col_1'=8,'col_2'=2] {'col_0','col_1'..., dimensions={0}, use_global_device_ids=true | all-gather | bytes 228096 | tf_op jit(solution)/shard_map/all_gather | solution.py:160
  238.4 1.9 reshape.209
  240.3 2.0 copy.47
  242.3 9.1 %all-gather.2 = f32[96,1152]{1,0:T(8,128)} all-gather(f32[48,1152]{1,0:T(8,128)} %bitcast.41), channel_id=4, replica_groups=mesh['row_0'=2,'row_1'=8,'col_0'=2,'col_1'=8,'col_2'=2] {'row_0'}, dimensions={0}, use_global_device_ids=true | all-gather | bytes 663552 | tf_op jit(solution)/shard_map/all_gather | solution.py:24
  251.3 2.2 copy.45
  253.6 1.9 gather_fusion.4
  255.6 1.2 broadcast_in_dim.114
  256.7 8.6 %all-to-all-start.1 = ((bf16[32,512,36]{1,2,0:T(8,128)(2,1)}), bf16[32,512,36]{1,2,0:T(8,128)(2,1)}, u32[]{:S(2)}, u32[]{:S(2)}) async-start(bf16[32,512,36]{1,2,0:T(8,128)(2,1)} %broadcast_in_dim.114), calls=%async_computation.1 | async-start | bytes 2621440 | tf_op jit(solution)/shard_map/all_to_all | solution.py:48
  266.3 35.4 %all-to-all-done.1 = bf16[32,512,36]{1,2,0:T(8,128)(2,1)} async-done(((bf16[32,512,36]{1,2,0:T(8,128)(2,1)}), bf16[32,512,36]{1,2,0:T(8,128)(2,1)}, u32[]{:S(2)}, u32[]{:S(2)}) %all-to-all-start.1) | async-done | bytes 1179680 | tf_op jit(solution)/shard_map/all_to_all | solution.py:48
  301.7 2.9 reshape.154
  304.6 4.8 %gather_fusion.5 = bf16[768,512]{1,0:T(8,128)(2,1)} fusion(bf16[512,1152]{0,1:T(8,128)(2,1)} %reshape.154, s32[1024]{0:T(1024)S(1)} %pad_clamp_fusion), kind=kCustom, calls=%fused_computation.5 | custom fusion | bytes 1575936 | tf_op jit(solution)/shard_map/jit(_take)/gather | solution.py:167
  309.4 2.2 broadcast_select_fusion.target_ref
  311.5 4.1 %copy.42 = f32[2,8,48,1152]{3,2,1,0:T(8,128)} copy(f32[2,8,48,1152]{3,2,0,1:T(8,128)} %bitcast.37) | data formatting | bytes 7077888 | tf_op jit(solution)/shard_map/transpose | solution.py:27
  315.6 5.2 %copy.43 = f32[768,1152]{0,1:T(8,128)} copy(f32[768,1152]{1,0:T(8,128)} %bitcast.36) | data formatting | bytes 7077888 | tf_op jit(solution)/shard_map/reshape;reshape | solution.py:18
  320.8 6.1 %gather_fusion.3 = f32[768,768]{1,0:T(8,128)} fusion(f32[768,1152]{0,1:T(8,128)} %copy.43, s32[1024]{0:T(1024)S(1)} %pad_clamp_fusion), kind=kCustom, calls=%fused_computation.3 | custom fusion | bytes 4721664 | tf_op jit(solution)/shard_map/jit(_take)/gather | solution.py:163
  326.9 3.3 select_bitcast_fusion
  330.2 3.1 copy.44
  333.3 2.8 add_multiply_fusion.matrix_ref
  336.1 54.6 %shard_map.55 = bf16[768,512]{1,0:T(8,128)(2,1)S(1)} custom-call(f32[768,768]{1,0:T(8,128)S(1)} %add_multiply_fusion.matrix_ref, bf16[768,512]{1,0:T(8,128)(2,1)S(1)} %copy-done.1), custom_call_target="tpu_custom_call" | custom-call | tf_op jit(solution)/shard_map/pallas_call | solution.py:135
  391.6 3.8 subtract_convert_fusion
  (35 shorter events, 6.8 us)
Async XLA Ops:
  6.5 1.9 copy-start
  6.5 59.6 %all-gather.12.cloned.1.call-start = ((), (), s32[]{:S(2)}) async-start(), calls=%async_computation.3 | async-start | bytes 2580480 | tf_op jit(solution)/shard_map/all_gather | solution.py:24
  17.7 73.5 %all-gather.14.cloned.1.call-start = ((), (), s32[]{:S(2)}) async-start(), calls=%async_computation.4 | async-start | bytes 6193152 | tf_op jit(solution)/shard_map/all_gather | solution.py:24
  66.1 4.7 %copy-start.3 = (s32[32]{0:T(128)S(1)}, s32[32]{0:T(128)}, u32[]{:S(2)}) copy-start(s32[32]{0:T(128)} %param.9) | copy-start | bytes 388
  70.7 240.8 %all-gather.16.cloned.1.call-start = ((), (), s32[]{:S(2)}) async-start(), calls=%async_computation.5 | async-start | bytes 3981312 | tf_op jit(solution)/shard_map/all_gather | solution.py:24
  256.7 44.9 %all-to-all-start.1 = ((bf16[32,512,36]{1,2,0:T(8,128)(2,1)}), bf16[32,512,36]{1,2,0:T(8,128)(2,1)}, u32[]{:S(2)}, u32[]{:S(2)}) async-start(bf16[32,512,36]{1,2,0:T(8,128)(2,1)} %broadcast_in_dim.114), calls=%async_computation.1 | async-start | bytes 2621440 | tf_op jit(solution)/shard_map/all_to_all | solution.py:48
  265.4 126.2 %all-gather.10.cloned.1.call-start = ((), (), s32[]{:S(2)}) async-start(), calls=%async_computation.2 | async-start | bytes 1462272 | tf_op jit(solution)/shard_map/all_gather | solution.py:171
  333.3 2.8 copy-start.1
  390.7 0.9 copy-start.2
Sparse Core Ops, SparseCore 0:
  17.9 48.2 all-gather.11
  70.8 20.3 all-gather.13
  251.5 45.8 all-gather.15
  299.3 71.6 all-gather.9

commit v2 on v1

--- a/solution.py
+++ b/solution.py
@@ -8,8 +8,10 @@
 from jax.sharding import PartitionSpec as P
 
 KDEV = 24
-COL = ("col_0", "col_1", "col_2")
-ROW = ("row_0", "row_1")
+COL = ("x_hi", "z", "core")
+ROW = ("x_lo", "y")
+MESH = pl.DeviceIdType.MESH
+ROWS16 = 48
 
 
 def laid_out(parts, dim):
@@ -43,19 +45,7 @@
     return arrived.sum(axis=0)
 
 
-def from_everyone(array, axis):
-    count = lax.axis_size(axis)
-    return lax.all_to_all(
-        jnp.broadcast_to(array[None], (count, *array.shape)), axis, 0, 0, tiled=True
-    )
-
-
-def gathered_copies(array, axis, dim):
-    parts = from_everyone(array, axis)
-    return laid_out(parts, dim)
-
-
-def compact_index(counts, removed_count, slot_count):
+def compact_index(counts, removed_count):
     shard_ids = jnp.arange(counts.shape[0], dtype=jnp.int32)
     shard_starts = jnp.sum(jnp.where(shard_ids[None, :] < shard_ids[:, None], counts[None, :], 0), axis=1)
     shard_ends = shard_starts + counts
@@ -64,7 +54,7 @@
     owner_start = jnp.sum(
         jnp.where(owners[:, None] == shard_ids[None, :], shard_starts[None, :], 0), axis=1
     )
-    return owners * slot_count + positions - owner_start
+    return owners, positions - owner_start
 
 
 HI = lax.Precision.HIGHEST
@@ -143,29 +133,182 @@
     )(matrix, targets)
 
 
+def remote(src, dst, sems, n, device):
+    send, recv = sems
+    return pltpu.make_async_remote_copy(
+        src_ref=src, dst_ref=dst, send_sem=send.at[n], recv_sem=recv.at[n],
+        device_id=device, device_id_type=MESH,
+    )
+
+
+def greet(devices):
+    barrier = pltpu.get_barrier_semaphore()
+    for device in devices:
+        pl.semaphore_signal(barrier, inc=1, device_id=device, device_id_type=MESH)
+    pl.semaphore_wait(barrier, len(devices))
+
+
+class Gather:
+    def __init__(self, source, out, sems, base, pair, ring, core, slot):
+        self.source, self.out, self.sems, self.base = source, out, sems, base
+        self.pair, self.ring, self.core, self.slot = pair, ring, core, slot
+        self.p, self.r = lax.axis_index(pair), lax.axis_index(ring)
+        self.k = lax.axis_index("core")
+        self.n = lax.axis_size(ring)
+        self.sent, self.number = [], {}
+
+    @staticmethod
+    def count(n, core):
+        return 1 + 2 * (n - 1) + (2 * n if core else 0)
+
+    def at(self, other, offset, sibling=False):
+        p = 1 - self.p if other else self.p
+        k = 1 - self.k if sibling else self.k
+        return self.out.at[self.slot(p, lax.rem(self.r + offset + self.n, self.n), k)]
+
+    def copy(self, name, src, dst, device):
+        n = self.number.setdefault(name, len(self.number))
+        return remote(src, dst, self.sems, self.base + n, device)
+
+    def send(self, name, block, device):
+        copy = self.copy(name, block[0], block[1], device)
+        copy.start()
+        self.sent.append(copy)
+
+    def arrived(self, name, dst, device):
+        self.copy(name, dst, dst, device).wait_recv()
+
+    def step(self, way):
+        return {self.ring: lax.rem(self.r + way + self.n, self.n)}
+
+    def share(self, other, offset, block):
+        if self.core:
+            self.send(("core", other, offset % self.n), block, {"core": 1 - self.k})
+
+    def begin(self):
+        own = (self.source, self.at(False, 0))
+        self.send("pair", own, {self.pair: 1 - self.p})
+        for way in (1, -1):
+            self.send((way, False, 1), own, self.step(way))
+        self.share(False, 0, own)
+
+    def spread_pair(self):
+        block = self.at(True, 0)
+        self.arrived("pair", block, {self.pair: 1 - self.p})
+        for way in (1, -1):
+            self.send((way, True, 1), (block, block), self.step(way))
+        self.share(True, 0, (block, block))
+
+    def advance(self, s):
+        half = self.n // 2
+        for other in (False, True):
+            for way in (1, -1):
+                last = half if (way == 1) != other else half - 1
+                if s > last:
+                    continue
+                block = self.at(other, -way * s)
+                self.arrived((way, other, s), block, self.step(way))
+                if s < last:
+                    self.send((way, other, s + 1), (block, block), self.step(way))
+                self.share(other, -way * s, (block, block))
+
+    def finish(self):
+        if self.core:
+            for other in (False, True):
+                for offset in range(self.n):
+                    self.arrived(("core", other, offset), self.at(other, offset, True), {"core": 1 - self.k})
+        for copy in self.sent:
+            copy.wait_send()
+
+    def run(self):
+        self.begin()
+        self.spread_pair()
+        for s in range(1, self.n // 2 + 1):
+            self.advance(s)
+        self.finish()
+
+
+def col_slot(p, r, k):
+    return (p * lax.axis_size("z") + r) * 2 + k
+
+
+def row_slot(p, r, k):
+    return p * lax.axis_size("y") + r
+
+
+def col_neighbours():
+    z, n = lax.axis_index("z"), lax.axis_size("z")
+    return [
+        {"core": 1 - lax.axis_index("core")},
+        {"x_hi": 1 - lax.axis_index("x_hi")},
+        {"z": lax.rem(z + 1, n)},
+        {"z": lax.rem(z + n - 1, n)},
+    ]
+
+
+def gather_col_kernel(block_ref, out_ref, send, recv, local):
+    mine = pltpu.make_async_copy(
+        block_ref, out_ref.at[col_slot(lax.axis_index("x_hi"), lax.axis_index("z"), lax.axis_index("core"))], local
+    )
+    mine.start()
+    greet(col_neighbours())
+    Gather(block_ref, out_ref, (send, recv), 0, "x_hi", "z", True, col_slot).run()
+    mine.wait()
+
+
+def gather_col(block):
+    n = Gather.count(lax.axis_size("z"), True)
+    return pl.pallas_call(
+        gather_col_kernel,
+        out_shape=jax.ShapeDtypeStruct((lax.axis_size(COL), *block.shape), block.dtype),
+        in_specs=[pl.BlockSpec(memory_space=pltpu.VMEM)],
+        out_specs=pl.BlockSpec(memory_space=pltpu.VMEM),
+        scratch_shapes=[pltpu.SemaphoreType.DMA((n,)), pltpu.SemaphoreType.DMA((n,)), pltpu.SemaphoreType.DMA],
+        compiler_params=pltpu.CompilerParams(collective_id=0, has_side_effects=True, vmem_limit_bytes=40 << 20),
+    )(block)
+
+
+def picked(positions, size):
+    return (positions[:, None] == jnp.arange(size, dtype=jnp.int32)[None, :]).astype(jnp.bfloat16)
+
+
+def exact_rows(choice, array, dims):
+    return lax.dot_general(choice, array, (dims, ((), ())), preferred_element_type=jnp.float32)
+
+
+def payload_of(eigenbasis, weight, local_picks):
+    slots, width = local_picks.shape[0], eigenbasis.shape[1]
+    basis_rows = jnp.take(eigenbasis, local_picks, axis=0)
+    columns = exact_rows(picked(local_picks, weight.shape[1]), weight, ((1,), (1,))).astype(jnp.bfloat16)
+    columns = columns.reshape(ROWS16 - slots, -1)
+    columns = jnp.pad(columns, ((0, 0), (0, width - columns.shape[1])))
+    return jnp.concatenate([basis_rows, columns], axis=0)
+
+
 def shards(weight, eigenbasis, eigenvalues, removed_local, counts):
     removed_count = KDEV * lax.axis_size(COL)
     slot_count = removed_local.shape[1]
     local_picks = removed_local[0]
-    compact_order = compact_index(counts, removed_count, slot_count)
-    chosen = jnp.take(eigenbasis, local_picks, axis=0).astype(jnp.float32)
-    scaled = (chosen / eigenvalues[None, :]).astype(jnp.bfloat16)
-    gathered = whole_of(scaled, COL, (0, 1, 2), 0)
-    compacted = jnp.take(gathered, compact_order, axis=0)
+    owners, ranks = compact_index(counts, removed_count)
+    gathered = gather_col(payload_of(eigenbasis, weight, local_picks))
+    shard_count, _, slab = gathered.shape
+    basis = exact_rows(picked(owners * ROWS16 + ranks, shard_count * ROWS16), gathered.reshape(-1, slab), ((1,), (0,)))
+    scaled = (basis / eigenvalues[None, :]).astype(jnp.bfloat16)
+    columns = gathered[:, slot_count:, : slot_count // (ROWS16 - slot_count) * weight.shape[0]]
+    targets = exact_rows(
+        picked(owners * slot_count + ranks, shard_count * slot_count), columns.reshape(-1, weight.shape[0]), ((1,), (0,))
+    ).astype(jnp.bfloat16)
     partial_value = lax.dot_general(
-        compacted, eigenbasis, (((1,), (1,)), ((), ())), preferred_element_type=jnp.float32
+        scaled, eigenbasis, (((1,), (1,)), ((), ())), preferred_element_type=jnp.float32
     )
     share = sum_at_owner(partial_value, ROW, 0)
     block_share = jnp.take(share, local_picks, axis=1)
     block_band = lax.all_gather(block_share, COL, axis=1, tiled=True)
     block_whole = whole_of(block_band, ROW, (0, 1), 0)
     share_half = share.astype(jnp.bfloat16)
-    block_matrix = jnp.take(block_whole, compact_order, axis=1)
+    block_matrix = jnp.take(block_whole, owners * slot_count + ranks, axis=1)
     block_matrix = 0.5 * (block_matrix + block_matrix.T)
-    weight_piece = jnp.take(weight, local_picks, axis=1)
-    everything = gathered_copies(weight_piece, COL, 1)
-    everything = jnp.take(everything, compact_order, axis=1)
-    solved_half = solve(block_matrix, everything.T)
+    solved_half = solve(block_matrix, targets)
     change = lax.dot_general(
         solved_half,
         lax.all_gather(share_half, ROW, axis=0, tiled=True),
@@ -176,7 +319,7 @@
 
 
 def solution(mesh):
-    torus = Mesh(mesh.devices.reshape(2, 8, 2, 8, 2), ("row_0", "row_1", "col_0", "col_1", "col_2"))
+    torus = Mesh(mesh.devices.reshape(2, 8, 2, 8, 2), ("x_lo", "y", "x_hi", "z", "core"))
     return jax.shard_map(
         shards,
         mesh=torus,

time: 403 us -> 340 us (0.84)
  the two profiles are of different devices: /device:TPU:64 before, /device:TPU:1 now
where the time goes in v2:
time: 340 us; the launch traced here: 339 us
  blocking collectives  126 us (37%)
  Pallas kernels  100 us (29%)
  local copies, waits for them, and re-layouts  35 us (10%)
  waiting for transfers between devices  31.6 us (9%)
  matrix products  20.2 us (6%)
  between operations  13.5 us (4%)
  other arithmetic  12.2 us (4%)
    all_to_all x1, blocking collectives, sum_at_owner(): lax.all_to_all(parts, axis, split_axis=0, concat_axis=0, tiled=True)  70.2 us
    pallas_call x1, Pallas kernels, solve(): pl.pallas_call(functools.partial(solve_kernel, nblk), out_shape=jax.Shape...  54.6 us
    all_gather x1, blocking collectives, shards(): block_band = lax.all_gather(block_share, COL, axis=1, tiled=True)  47.4 us
    pallas_call x1, Pallas kernels, gather_col(): pl.pallas_call(gather_col_kernel, out_shape=jax.ShapeDtypeStruct((lax.axi...  45.7 us
    all_gather x1, waiting for transfers between devices, gather_in_order(): parts = lax.all_gather(parts, axes[k])  31.5 us
    dot_general x1, matrix products, shards(): lax.dot_general(scaled, eigenbasis, (((1,), (1,)), ((), ())), preferred_e...  11.5 us
    all_gather x1, blocking collectives, gather_in_order(): parts = lax.all_gather(parts, axes[k])  8.71 us
    unnamed x12, local copies, waits for them, and re-layouts  7.18 us
  transfers between devices with their start and end apart: 2, of which 1 were waited for; matrix products, arithmetic and copies ran while one was open for 10% of the time, Pallas kernels for 16%

profile of v2, /device:TPU:1, one launch (start us, length us, event | category | flops | bytes accessed | tf_op | source)
XLA Modules:
  0.0 339.3 jit_solution(17821012696774115344)
XLA Ops:
  6.5 0.8 compare_and_fusion.1
  7.4 0.8 fusion.11
  8.2 0.8 select_reduce_fusion.1
  8.9 0.7 add.79
  9.8 1.6 convolution_convert_fusion
  11.5 0.7 gather_fusion
  12.3 45.7 %shard_map.55 = bf16[32,48,1792]{2,1,0:T(8,128)(2,1)S(1)} custom-call(bf16[48,1792]{1,0:T(8,128)(2,1)S(1)} %fusion.7.block_ref), custom_call_target="tpu_custom_call" | custom-call | tf_op jit(solution)/shard_map/pallas_call | solution.py:261
  58.0 2.4 copy-done.1
  60.3 11.5 %fusion.5 = f32[768,896]{1,0:T(8,128)} fusion(bf16[896,1792]{1,0:T(8,128)(2,1)S(1)} %copy-done, bf16[1536,1792]{1,0:T(8,128)(2,1)} %bitcast.24, f32[1792]{0:T(1024)S(1)} %copy-done.4, s32[768]{0:T(1024)S(1)} %get-tuple-element.8), kind=kOutput, calls=%fused_computation.15 | convolution fusion | flops 6698041344 | bytes 11479040 | tf_op jit(solution)/shard_map/dot_general | solution.py:301
  71.9 70.2 %all_to_all.5 = f32[16,48,896]{2,1,0:T(8,128)} all-to-all(f32[16,48,896]{2,1,0:T(8,128)} %bitcast.27), channel_id=1, replica_groups=mesh['x_lo'=2,'y'=8,'x_hi'=2,'z'=8,'core'=2] {'x_lo','y'}, dimensions={0} | all-to-all | bytes 5505024 | tf_op jit(solution)/shard_map/all_to_all | solution.py:44
  142.0 1.9 reduce_sum.41
  143.9 1.0 copy.16
  144.9 1.6 gather_fusion.1
  146.6 47.4 %all-gather.2 = f32[32,36,48]{2,1,0:T(8,128)} all-gather(f32[1,36,48]{2,1,0:T(8,128)S(1)} %select_bitcast_fusion.1), channel_id=1, replica_groups=mesh['x_lo'=2,'y'=8,'x_hi'=2,'z'=8,'core'=2] {'x_hi','z','core'}, dimensions={0}, use_global_device_ids=true | all-gather | bytes 228096 | tf_op jit(solution)/shard_map/all_gather | solution.py:306
  194.0 1.9 reshape.137
  196.0 2.0 copy.21
  197.9 8.7 %all-gather = f32[96,1152]{1,0:T(8,128)} all-gather(f32[48,1152]{1,0:T(8,128)} %bitcast.29), channel_id=2, replica_groups=mesh['x_lo'=2,'y'=8,'x_hi'=2,'z'=8,'core'=2] {'x_lo'}, dimensions={0}, use_global_device_ids=true | all-gather | bytes 663552 | tf_op jit(solution)/shard_map/all_gather | solution.py:26
  206.7 0.2 all-gather.6.cloned.1.call-start
  206.9 0.6 convert_element_type.31
  207.6 3.0 slice.3
  210.6 3.3 reshape.108
  213.9 3.4 fusion.4.target_ref
  217.3 31.5 %all-gather.8.cloned.1.call-done = f32[16,48,1152]{2,1,0:T(8,128)} async-done(((f32[2,48,1152]{2,1,0:T(8,128)}), f32[16,48,1152]{2,1,0:T(8,128)}) %all-gather.8.cloned.1.call-update) | async-done | bytes 3538960 | tf_op jit(solution)/shard_map/all_gather | solution.py:26
  248.8 4.0 %copy.18 = f32[2,8,48,1152]{3,2,1,0:T(8,128)} copy(f32[2,8,48,1152]{3,2,0,1:T(8,128)} %bitcast.26) | data formatting | bytes 7077888 | tf_op jit(solution)/shard_map/transpose | solution.py:29
  252.8 5.2 %copy.19 = f32[768,1152]{0,1:T(8,128)} copy(f32[768,1152]{1,0:T(8,128)} %bitcast.25) | data formatting | bytes 7077888 | tf_op jit(solution)/shard_map/reshape;reshape | solution.py:20
  258.0 6.1 %gather_fusion.2 = f32[768,768]{1,0:T(8,128)} fusion(f32[768,1152]{0,1:T(8,128)} %copy.19, s32[1024]{0:T(1024)S(1)} %pad_clamp_fusion), kind=kCustom, calls=%fused_computation.2 | custom fusion | bytes 4721664 | tf_op jit(solution)/shard_map/jit(_take)/gather | solution.py:309
  264.1 3.3 select_bitcast_fusion
  267.4 3.0 copy.20
  270.5 2.8 add_multiply_fusion.matrix_ref
  273.3 54.6 %shard_map.56 = bf16[768,512]{1,0:T(8,128)(2,1)S(1)} custom-call(f32[768,768]{1,0:T(8,128)S(1)} %add_multiply_fusion.matrix_ref, bf16[768,512]{1,0:T(8,128)(2,1)S(1)} %copy-done.2), custom_call_target="tpu_custom_call" | custom-call | tf_op jit(solution)/shard_map/pallas_call | solution.py:125
  327.9 0.9 copy-done.3
  328.7 3.8 %subtract_convert_fusion = bf16[512,896]{1,0:T(8,128)(2,1)} fusion(bf16[512,896]{1,0:T(8,128)(2,1)} %param.5, bf16[768,512]{1,0:T(8,128)(2,1)} %copy-done.3, bf16[768,896]{1,0:T(8,128)(2,1)} %all-gather.6.cloned.1.call-done), kind=kOutput, calls=%fused_computation.11 | convolution fusion | flops 706019328 | bytes 3997696 | tf_op jit(solution)/shard_map/dot_general | solution.py:312
  (23 shorter events, 0.5 us)
Async XLA Ops:
  6.5 4.9 %copy-start = (bf16[896,1792]{1,0:T(8,128)(2,1)S(1)}, bf16[896,1792]{1,0:T(8,128)(2,1)}, u32[]{:S(2)}) copy-start(bf16[896,1792]{1,0:T(8,128)(2,1)} %param.6) | copy-start | bytes 9633796
  6.5 242.3 %all-gather.8.cloned.1.call-start = ((), (), s32[]{:S(2)}) async-start(), calls=%async_computation.2 | async-start | bytes 3981312 | tf_op jit(solution)/shard_map/all_gather | solution.py:26
  12.2 48.1 %copy-start.4 = (f32[1792]{0:T(1024)S(1)}, f32[1792]{0:T(1024)}, u32[]{:S(2)}) copy-start(f32[1792]{0:T(1024)} %param.7) | copy-start | bytes 21508
  58.0 2.4 copy-start.1
  206.7 122.1 %all-gather.6.cloned.1.call-start = ((), (), s32[]{:S(2)}) async-start(), calls=%async_computation.1 | async-start | bytes 1462272 | tf_op jit(solution)/shard_map/all_gather | solution.py:314
  270.5 2.8 copy-start.2
  327.9 0.9 copy-start.3
Sparse Core Ops, SparseCore 0:
  206.8 41.9 all-gather.7
  250.9 61.7 all-gather.5

commit v3 on v2

--- a/solution.py
+++ b/solution.py
@@ -12,37 +12,6 @@
 ROW = ("x_lo", "y")
 MESH = pl.DeviceIdType.MESH
 ROWS16 = 48
-
-
-def laid_out(parts, dim):
-    dims = list(parts.shape[1:])
-    dims[dim] *= parts.shape[0]
-    return jnp.moveaxis(parts, 0, dim).reshape(dims)
-
-
-def gather_in_order(array, axes, sequence):
-    parts = array
-    for k in sequence:
-        parts = lax.all_gather(parts, axes[k])
-    done = sequence[::-1]
-    back = [done.index(k) for k in range(len(axes))]
-    parts = parts.transpose(*back, *range(len(axes), parts.ndim))
-    return parts.reshape(-1, *array.shape)
-
-
-def whole_of(array, axes, sequence, dim):
-    return laid_out(gather_in_order(array, axes, sequence), dim)
-
-
-def split_up(array, dim, count):
-    before, after = (array.shape[:dim], array.shape[dim + 1 :])
-    return jnp.moveaxis(array.reshape(*before, count, -1, *after), dim, 0)
-
-
-def sum_at_owner(array, axis, dim):
-    parts = split_up(array, dim, lax.axis_size(axis))
-    arrived = lax.all_to_all(parts, axis, split_axis=0, concat_axis=0, tiled=True)
-    return arrived.sum(axis=0)
 
 
 def compact_index(counts, removed_count):
@@ -134,9 +103,8 @@
 
 
 def remote(src, dst, sems, n, device):
-    send, recv = sems
     return pltpu.make_async_remote_copy(
-        src_ref=src, dst_ref=dst, send_sem=send.at[n], recv_sem=recv.at[n],
+        src_ref=src, dst_ref=dst, send_sem=sems[0].at[n], recv_sem=sems[1].at[n],
         device_id=device, device_id_type=MESH,
     )
 
@@ -149,8 +117,8 @@
 
 
 class Gather:
-    def __init__(self, source, out, sems, base, pair, ring, core, slot):
-        self.source, self.out, self.sems, self.base = source, out, sems, base
+    def __init__(self, source, out, sems, pair, ring, core, slot):
+        self.source, self.out, self.sems = source, out, sems
         self.pair, self.ring, self.core, self.slot = pair, ring, core, slot
         self.p, self.r = lax.axis_index(pair), lax.axis_index(ring)
         self.k = lax.axis_index("core")
@@ -166,38 +134,40 @@
         k = 1 - self.k if sibling else self.k
         return self.out.at[self.slot(p, lax.rem(self.r + offset + self.n, self.n), k)]
 
-    def copy(self, name, src, dst, device):
+    def device(self, name):
+        if name[0] == "pair":
+            return {self.pair: 1 - self.p}
+        if name[0] == "core":
+            return {"core": 1 - self.k}
+        return {self.ring: lax.rem(self.r + name[0] + self.n, self.n)}
+
+    def copy(self, name, other, offset, own=False):
+        block = self.at(other, offset)
         n = self.number.setdefault(name, len(self.number))
-        return remote(src, dst, self.sems, self.base + n, device)
-
-    def send(self, name, block, device):
-        copy = self.copy(name, block[0], block[1], device)
-        copy.start()
-        self.sent.append(copy)
-
-    def arrived(self, name, dst, device):
-        self.copy(name, dst, dst, device).wait_recv()
-
-    def step(self, way):
-        return {self.ring: lax.rem(self.r + way + self.n, self.n)}
-
-    def share(self, other, offset, block):
+        return remote(self.source if own else block, block, self.sems, n, self.device(name))
+
+    def send(self, *what):
+        self.copy(*what).start()
+        self.sent.append(what)
+
+    def arrived(self, name, dst):
+        remote(dst, dst, self.sems, self.number[name], self.device(name)).wait_recv()
+
+    def share(self, other, offset, own=False):
         if self.core:
-            self.send(("core", other, offset % self.n), block, {"core": 1 - self.k})
+            self.send(("core", other, offset % self.n), other, offset, own)
 
     def begin(self):
-        own = (self.source, self.at(False, 0))
-        self.send("pair", own, {self.pair: 1 - self.p})
+        self.send(("pair",), False, 0, True)
         for way in (1, -1):
-            self.send((way, False, 1), own, self.step(way))
-        self.share(False, 0, own)
+            self.send((way, False, 1), False, 0, True)
+        self.share(False, 0, True)
 
     def spread_pair(self):
-        block = self.at(True, 0)
-        self.arrived("pair", block, {self.pair: 1 - self.p})
+        self.arrived(("pair",), self.at(True, 0))
         for way in (1, -1):
-            self.send((way, True, 1), (block, block), self.step(way))
-        self.share(True, 0, (block, block))
+            self.send((way, True, 1), True, 0)
+        self.share(True, 0)
 
     def advance(self, s):
         half = self.n // 2
@@ -206,26 +176,22 @@
                 last = half if (way == 1) != other else half - 1
                 if s > last:
                     continue
-                block = self.at(other, -way * s)
-                self.arrived((way, other, s), block, self.step(way))
+                self.arrived((way, other, s), self.at(other, -way * s))
                 if s < last:
-                    self.send((way, other, s + 1), (block, block), self.step(way))
-                self.share(other, -way * s, (block, block))
+                    self.send((way, other, s + 1), other, -way * s)
+                self.share(other, -way * s)
 
     def finish(self):
         if self.core:
             for other in (False, True):
                 for offset in range(self.n):
-                    self.arrived(("core", other, offset), self.at(other, offset, True), {"core": 1 - self.k})
-        for copy in self.sent:
-            copy.wait_send()
-
-    def run(self):
-        self.begin()
-        self.spread_pair()
-        for s in range(1, self.n // 2 + 1):
-            self.advance(s)
-        self.finish()
+                    self.arrived(("core", other, offset), self.at(other, offset, True))
+        for what in self.sent:
+            self.copy(*what).wait_send()
+
+    def stages(self):
+        rest = [functools.partial(self.advance, s) for s in range(1, self.n // 2 + 1)]
+        return [self.begin, self.spread_pair, *rest, self.finish]
 
 
 def col_slot(p, r, k):
@@ -246,26 +212,191 @@
     ]
 
 
+def col_here():
+    return col_slot(lax.axis_index("x_hi"), lax.axis_index("z"), lax.axis_index("core"))
+
+
+def dma_pair(*shape):
+    return [pltpu.SemaphoreType.DMA(shape), pltpu.SemaphoreType.DMA(shape)]
+
+
 def gather_col_kernel(block_ref, out_ref, send, recv, local):
-    mine = pltpu.make_async_copy(
-        block_ref, out_ref.at[col_slot(lax.axis_index("x_hi"), lax.axis_index("z"), lax.axis_index("core"))], local
-    )
+    mine = pltpu.make_async_copy(block_ref, out_ref.at[col_here()], local)
     mine.start()
     greet(col_neighbours())
-    Gather(block_ref, out_ref, (send, recv), 0, "x_hi", "z", True, col_slot).run()
+    for stage in Gather(block_ref, out_ref, (send, recv), "x_hi", "z", True, col_slot).stages():
+        stage()
     mine.wait()
 
 
 def gather_col(block):
-    n = Gather.count(lax.axis_size("z"), True)
     return pl.pallas_call(
         gather_col_kernel,
         out_shape=jax.ShapeDtypeStruct((lax.axis_size(COL), *block.shape), block.dtype),
         in_specs=[pl.BlockSpec(memory_space=pltpu.VMEM)],
         out_specs=pl.BlockSpec(memory_space=pltpu.VMEM),
-        scratch_shapes=[pltpu.SemaphoreType.DMA((n,)), pltpu.SemaphoreType.DMA((n,)), pltpu.SemaphoreType.DMA],
+        scratch_shapes=[*dma_pair(Gather.count(lax.axis_size("z"), True)), pltpu.SemaphoreType.DMA],
         compiler_params=pltpu.CompilerParams(collective_id=0, has_side_effects=True, vmem_limit_bytes=40 << 20),
     )(block)
+
+
+class RowSum:
+    def __init__(self, partial, ring_in, last_in, done, ring_sems, last_sems, parts):
+        self.partial, self.ring_in, self.last_in, self.done = partial, ring_in, last_in, done
+        self.ring_sems, self.last_sems = ring_sems, last_sems
+        self.x, self.y, self.n = lax.axis_index("x_lo"), lax.axis_index("y"), lax.axis_size("y")
+        rows = partial.shape[1] // parts
+        self.cuts = [pl.ds(u * rows, rows) for u in range(parts)]
+
+    def term(self, w, hops, u):
+        way = 1 - 2 * w
+        return self.partial.at[w * self.n + lax.rem(self.y - way * hops + 2 * self.n, self.n), self.cuts[u]]
+
+    def copy(self, w, u, s):
+        src = self.term(w, 1, u) if s == 0 else self.ring_in.at[w, s - 1, self.cuts[u]]
+        n = (w * len(self.cuts) + u) * (self.n - 1) + s
+        target = {"y": lax.rem(self.y + 1 - 2 * w + self.n, self.n)}
+        return remote(src, self.ring_in.at[w, s, self.cuts[u]], self.ring_sems, n, target)
+
+    def every(self):
+        return [(w, u) for u in range(len(self.cuts)) for w in range(2)]
+
+    def begin(self):
+        for w, u in self.every():
+            self.copy(w, u, 0).start()
+
+    def advance(self, s):
+        for w, u in self.every():
+            self.copy(w, u, s).wait_recv()
+            self.ring_in[w, s, self.cuts[u]] += self.term(w, 2 + s, u)[...]
+            if s < self.n - 2:
+                self.copy(w, u, s + 1).start()
+
+    def last(self):
+        return remote(self.ring_in.at[1 - self.x, self.n - 2], self.last_in, self.last_sems, 0, {"x_lo": 1 - self.x})
+
+    def cross(self):
+        self.last().start()
+
+    def finish(self):
+        self.last().wait_recv()
+        self.done[row_slot(self.x, self.y, 0)] = (self.ring_in[self.x, self.n - 2] + self.last_in[...]).astype(jnp.bfloat16)
+        for w, u in self.every():
+            for s in range(self.n - 1):
+                self.copy(w, u, s).wait_send()
+        self.last().wait_send()
+
+    def stages(self):
+        return [self.begin, *[functools.partial(self.advance, s) for s in range(self.n - 1)], self.cross, self.finish]
+
+
+class BandSum:
+    def __init__(self, band, band_in, total, in_sems, out_sems):
+        self.band, self.band_in, self.total = band, band_in, total
+        self.in_sems, self.out_sems = in_sems, out_sems
+        self.x, self.y, self.n = lax.axis_index("x_lo"), lax.axis_index("y"), lax.axis_size("y")
+        self.bands = band.shape[1] // NB
+
+    def peers(self):
+        return [
+            (lax.rem(self.x + dx, 2), lax.rem(self.y + dy, self.n))
+            for dx in range(2) for dy in range(self.n) if dx or dy
+        ]
+
+    def home(self, p):
+        return jnp.logical_and(self.x == p % 2, self.y == p)
+
+    def inward(self, p, source):
+        target = {"x_lo": jnp.int32(p % 2), "y": jnp.int32(p)}
+        return pltpu.make_async_remote_copy(
+            src_ref=self.band.at[:, pl.ds(p * NB, NB)], dst_ref=self.band_in.at[source],
+            send_sem=self.in_sems[0].at[p], recv_sem=self.in_sems[1].at[source], device_id=target, device_id_type=MESH,
+        )
+
+    def outward(self, p, number, peer):
+        cut = self.total.at[:, pl.ds(p * NB, NB)]
+        return pltpu.make_async_remote_copy(
+            src_ref=cut, dst_ref=cut, send_sem=self.out_sems[0].at[number], recv_sem=self.out_sems[1].at[p],
+            device_id={"x_lo": peer[0], "y": peer[1]}, device_id_type=MESH,
+        )
+
+    def run(self):
+        here = row_slot(self.x, self.y, 0)
+        for p in range(self.bands):
+            @pl.when(jnp.logical_not(self.home(p)))
+            def _():
+                self.inward(p, here).start()
+        for p in range(self.bands):
+            @pl.when(self.home(p))
+            def _():
+                total = self.band[:, p * NB : (p + 1) * NB]
+                for x, y in self.peers():
+                    source = row_slot(x, y, 0)
+                    self.inward(p, source).wait_recv()
+                    total = total + self.band_in[source]
+                self.total[:, p * NB : (p + 1) * NB] = total
+                for number, peer in enumerate(self.peers()):
+                    self.outward(p, number, peer).start()
+        for p in range(self.bands):
+            @pl.when(jnp.logical_not(self.home(p)))
+            def _():
+                self.outward(p, 0, (jnp.int32(p % 2), jnp.int32(p))).wait_recv()
+
+    def finish(self):
+        here = row_slot(self.x, self.y, 0)
+        for p in range(self.bands):
+            @pl.when(jnp.logical_not(self.home(p)))
+            def _():
+                self.inward(p, here).wait_send()
+
+            @pl.when(self.home(p))
+            def _():
+                for number, peer in enumerate(self.peers()):
+                    self.outward(p, number, peer).wait_send()
+
+
+def reduce_kernel(band_ref, partial_ref, matrix_ref, rows_ref, band_in, total, ring_in, last_in, *sems):
+    pairs = [(sems[2 * i], sems[2 * i + 1]) for i in range(len(sems) // 2)]
+    band = BandSum(band_ref, band_in, total, pairs[0], pairs[1])
+    rows = RowSum(partial_ref, ring_in, last_in, rows_ref, pairs[2], pairs[3], 2)
+    spread = Gather(total, matrix_ref, pairs[4], "x_hi", "z", True, col_slot)
+    halves = Gather(rows_ref.at[row_slot(rows.x, rows.y, 0)], rows_ref, pairs[5], "x_lo", "y", False, row_slot)
+    greet([{"x_lo": x, "y": y} for x, y in band.peers()] + col_neighbours())
+    band.run()
+    matrix_ref[col_here()] = total[...]
+    first, second = spread.stages(), rows.stages() + halves.stages()
+    for i in range(max(len(first), len(second))):
+        if i < len(first):
+            first[i]()
+        if i < len(second):
+            second[i]()
+    band.finish()
+
+
+def reduce_rows(band, partial):
+    n, height, width = partial.shape
+    ny, nz = lax.axis_size("y"), lax.axis_size("z")
+    bands = band.shape[1] // NB
+    return pl.pallas_call(
+        reduce_kernel,
+        out_shape=[
+            jax.ShapeDtypeStruct((lax.axis_size(COL), *band.shape), jnp.float32),
+            jax.ShapeDtypeStruct(partial.shape, jnp.bfloat16),
+        ],
+        in_specs=[pl.BlockSpec(memory_space=pltpu.VMEM)] * 2,
+        out_specs=[pl.BlockSpec(memory_space=pltpu.VMEM)] * 2,
+        scratch_shapes=[
+            pltpu.VMEM((n, band.shape[0], NB), jnp.float32),
+            pltpu.VMEM(band.shape, jnp.float32),
+            pltpu.VMEM((2, ny - 1, height, width), jnp.float32),
+            pltpu.VMEM((height, width), jnp.float32),
+            pltpu.SemaphoreType.DMA((bands,)), pltpu.SemaphoreType.DMA((n,)),
+            pltpu.SemaphoreType.DMA((n - 1,)), pltpu.SemaphoreType.DMA((bands,)),
+            *dma_pair(4 * (ny - 1)), *dma_pair(1),
+            *dma_pair(Gather.count(nz, True)), *dma_pair(Gather.count(ny, False)),
+        ],
+        compiler_params=pltpu.CompilerParams(collective_id=1, has_side_effects=True, vmem_limit_bytes=48 << 20),
+    )(band, partial)
 
 
 def picked(positions, size):
@@ -292,29 +423,22 @@
     owners, ranks = compact_index(counts, removed_count)
     gathered = gather_col(payload_of(eigenbasis, weight, local_picks))
     shard_count, _, slab = gathered.shape
-    basis = exact_rows(picked(owners * ROWS16 + ranks, shard_count * ROWS16), gathered.reshape(-1, slab), ((1,), (0,)))
+    compact = picked(owners * ROWS16 + ranks, shard_count * ROWS16)
+    basis = exact_rows(compact, gathered.reshape(-1, slab), ((1,), (0,)))
     scaled = (basis / eigenvalues[None, :]).astype(jnp.bfloat16)
+    basis = basis.astype(jnp.bfloat16)
     columns = gathered[:, slot_count:, : slot_count // (ROWS16 - slot_count) * weight.shape[0]]
     targets = exact_rows(
         picked(owners * slot_count + ranks, shard_count * slot_count), columns.reshape(-1, weight.shape[0]), ((1,), (0,))
     ).astype(jnp.bfloat16)
-    partial_value = lax.dot_general(
-        scaled, eigenbasis, (((1,), (1,)), ((), ())), preferred_element_type=jnp.float32
-    )
-    share = sum_at_owner(partial_value, ROW, 0)
-    block_share = jnp.take(share, local_picks, axis=1)
-    block_band = lax.all_gather(block_share, COL, axis=1, tiled=True)
-    block_whole = whole_of(block_band, ROW, (0, 1), 0)
-    share_half = share.astype(jnp.bfloat16)
-    block_matrix = jnp.take(block_whole, owners * slot_count + ranks, axis=1)
-    block_matrix = 0.5 * (block_matrix + block_matrix.T)
-    solved_half = solve(block_matrix, targets)
-    change = lax.dot_general(
-        solved_half,
-        lax.all_gather(share_half, ROW, axis=0, tiled=True),
-        (((0,), (0,)), ((), ())),
-        preferred_element_type=jnp.float32,
-    )
+    first = lax.axis_index(COL) * KDEV
+    band = exact_rows(lax.dynamic_slice_in_dim(scaled, first, KDEV), basis, ((1,), (1,)))
+    band += exact_rows(lax.dynamic_slice_in_dim(basis, first, KDEV), scaled, ((1,), (1,)))
+    partial = exact_rows(scaled, eigenbasis, ((1,), (1,)))
+    row_count = lax.axis_size(ROW)
+    matrix, rows = reduce_rows(0.5 * band, partial.reshape(row_count, -1, partial.shape[1]))
+    solved_half = solve(matrix.reshape(removed_count, removed_count), targets)
+    change = exact_rows(solved_half, rows.reshape(removed_count, -1), ((0,), (0,)))
     return (weight.astype(jnp.float32) - change).astype(jnp.bfloat16)
 
 

time: 340 us -> 206 us (0.61)
  the two profiles are of different devices: /device:TPU:1 before, /device:TPU:2 now
where the time goes in v3:
time: 206 us; the launch traced here: 205 us
  Pallas kernels  176 us (85%)
  matrix products  17.4 us (8%)
  local copies, waits for them, and re-layouts  8.24 us (4%)
  other arithmetic  3.25 us (2%)
    pallas_call x1, Pallas kernels, reduce_rows(): pl.pallas_call(reduce_kernel, out_shape=[jax.ShapeDtypeStruct((lax.axis_s...  78.8 us
    pallas_call x1, Pallas kernels, solve(): pl.pallas_call(functools.partial(solve_kernel, nblk), out_shape=jax.Shape...  54.3 us
    pallas_call x1, Pallas kernels, gather_col(): pl.pallas_call(gather_col_kernel, out_shape=jax.ShapeDtypeStruct((lax.axi...  43.3 us
    dot_general x7, matrix products, exact_rows(): lax.dot_general(choice, array, (dims, ((), ())), preferred_element_type=j...  17.4 us

profile of v3, /device:TPU:2, one launch (start us, length us, event | category | flops | bytes accessed | tf_op | source)
XLA Modules:
  0.0 205.4 jit_solution(5477447839385017540)
XLA Ops:
  0.0 0.0 copy-start
  0.0 0.9 select_reduce_fusion.1
  0.9 0.7 add.53
  1.6 0.7 compare_and_fusion
  2.3 0.7 fusion.12
  3.0 0.1 convert_reduce_fusion
  3.0 0.1 select_reduce_fusion
  3.2 1.6 convolution_convert_fusion
  4.8 0.0 copy-done
  4.8 0.7 gather_fusion
  5.5 0.1 broadcast_select_fusion
  5.6 43.3 %shard_map.55 = bf16[32,48,1792]{2,1,0:T(8,128)(2,1)S(1)} custom-call(bf16[48,1792]{1,0:T(8,128)(2,1)S(1)} %fusion.7.block_ref), custom_call_target="tpu_custom_call" | custom-call | tf_op jit(solution)/shard_map/pallas_call | solution.py:233
  48.9 0.0 copy-start.1
  48.9 2.4 %copy-done.1 = bf16[32,48,1792]{2,1,0:T(8,128)(2,1)} copy-done((bf16[32,48,1792]{2,1,0:T(8,128)(2,1)}, bf16[32,48,1792]{2,1,0:T(8,128)(2,1)S(1)}, u32[]{:S(2)}) %copy-start.1) | copy-done | bytes 5505048
  51.2 1.6 slice.3
  52.9 3.3 %reshape.80 = bf16[1152,512]{1,0:T(8,128)(2,1)} reshape(bf16[32,12,1536]{2,1,0:T(8,128)(2,1)} %slice.3) | data formatting | bytes 2359296 | tf_op jit(solution)/shard_map/reshape | solution.py:432
  56.1 0.0 copy-start.2
  56.1 0.0 copy-start.4
  56.1 2.6 %fusion.4.target_ref = bf16[768,512]{1,0:T(8,128)(2,1)S(1)} fusion(bf16[1152,512]{1,0:T(8,128)(2,1)} %reshape.80, s32[768]{0:T(1024)S(1)} %get-tuple-element.11), kind=kOutput, calls=%fused_computation.9 | convolution fusion | flops 907247616 | bytes 1969152 | tf_op jit(solution)/shard_map/dot_general | solution.py:407
  58.8 0.3 copy-done.2
  59.1 0.0 copy-done.4
  59.1 4.9 %divide_convert_fusion = (bf16[768,1792]{1,0:T(8,128)(2,1)S(1)}, bf16[768,1792]{1,0:T(8,128)(2,1)S(1)}) fusion(f32[1792]{0:T(1024)S(1)} %copy-done.4, bf16[1536,1792]{1,0:T(8,128)(2,1)S(1)} %bitcast.19, s32[768]{0:T(1024)S(1)} %get-tuple-element.12), kind=kOutput, calls=%fused_computation.1 | convolution fusion | flops 4233166848 | bytes 11020288 | tf_op jit(solution)/shard_map/dot_general | solution.py:407
  63.9 0.8 fusion.9
  64.8 0.9 fusion.5.band_ref
  65.7 4.6 %fusion.15 = f32[768,896]{1,0:T(8,128)} fusion(bf16[768,1792]{1,0:T(8,128)(2,1)S(1)} %get-tuple-element.9, bf16[896,1792]{1,0:T(8,128)(2,1)S(1)} %copy-done), kind=kOutput, calls=%fused_computation.38 | convolution fusion | flops 2466250752 | bytes 8716288 | tf_op jit(solution)/shard_map/dot_general | solution.py:407
  70.3 0.0 copy-start.3
  70.3 78.8 %shard_map.56 = (f32[32,24,768]{2,1,0:T(8,128)S(1)}, bf16[16,48,896]{2,1,0:T(8,128)(2,1)S(1)}) custom-call(f32[24,768]{1,0:T(8,128)S(1)} %fusion.5.band_ref, f32[16,48,896]{2,1,0:T(8,128)} %bitcast.22), custom_call_target="tpu_custom_call" | custom-call | tf_op jit(solution)/shard_map/pallas_call | solution.py:380
  149.1 54.3 %shard_map.57 = bf16[768,512]{1,0:T(8,128)(2,1)S(1)} custom-call(f32[768,768]{1,0:T(8,128)S(1)} %bitcast.20, bf16[768,512]{1,0:T(8,128)(2,1)S(1)} %fusion.4.target_ref), custom_call_target="tpu_custom_call" | custom-call | tf_op jit(solution)/shard_map/pallas_call | solution.py:94
  203.5 0.0 copy-done.3
  203.5 1.9 subtract_convert_fusion
  (4 shorter events, 0.1 us)
Async XLA Ops:
  0.0 4.8 %copy-start = (bf16[896,1792]{1,0:T(8,128)(2,1)S(1)}, bf16[896,1792]{1,0:T(8,128)(2,1)}, u32[]{:S(2)}) copy-start(bf16[896,1792]{1,0:T(8,128)(2,1)} %param.6) | copy-start | bytes 9633796
  48.9 2.4 %copy-start.1 = (bf16[32,48,1792]{2,1,0:T(8,128)(2,1)}, bf16[32,48,1792]{2,1,0:T(8,128)(2,1)S(1)}, u32[]{:S(2)}) copy-start(bf16[32,48,1792]{2,1,0:T(8,128)(2,1)S(1)} %shard_map.55) | copy-start | bytes 16515076
  56.1 2.9 %copy-start.2 = (bf16[32,48,1792]{2,1,0:T(8,128)(2,1)S(1)}, bf16[32,48,1792]{2,1,0:T(8,128)(2,1)}, u32[]{:S(2)}) copy-start(bf16[32,48,1792]{2,1,0:T(8,128)(2,1)} %copy-done.1) | copy-start | bytes 16515076
  56.1 2.9 %copy-start.4 = (f32[1792]{0:T(1024)S(1)}, f32[1792]{0:T(1024)}, u32[]{:S(2)}) copy-start(f32[1792]{0:T(1024)} %param.7) | copy-start | bytes 21508
  70.3 133.2 %copy-start.3 = (bf16[512,896]{1,0:T(8,128)(2,1)S(1)}, bf16[512,896]{1,0:T(8,128)(2,1)}, u32[]{:S(2)}) copy-start(bf16[512,896]{1,0:T(8,128)(2,1)} %param.5) | copy-start | bytes 2752516

commit v4 on v3

--- a/solution.py
+++ b/solution.py
@@ -60,46 +60,51 @@
                 tiles[i] = t - parts[0]
     return jnp.concatenate(tiles, axis=0)
 
-def solve_kernel(nblk, matrix_ref, target_ref, out_ref, aug, upper, sol):
-    width = nblk * NB
-    for i in range(nblk):
-        aug[i, :, :width] = matrix_ref[i * NB : (i + 1) * NB, :]
-        aug[i, :, width:] = target_ref[i * NB : (i + 1) * NB, :].astype(jnp.float32)
+def load_system(count, matrix, targets, aug):
+    width = count * NB
+    for i in range(count):
+        aug[i, :, :width] = matrix[i * NB : (i + 1) * NB, :]
+        aug[i, :, width:] = targets[i * NB : (i + 1) * NB, :].astype(jnp.float32)
+
+
+def solve_system(count, out, aug, upper, sol, beside):
+    width = count * NB
+
+    def pause(k, which):
+        for i in range(count):
+            if 2 * i + which < len(beside):
+                @pl.when(k == i)
+                def _():
+                    for call in beside[2 * i + which]:
+                        call()
 
     def eliminate(k, _):
         here = pl.ds(pl.multiple_of(k * NB, NB), NB)
         inverse = invert_block(aug[k, :, here])
-        panel = jnp.dot(inverse, aug[k], preferred_element_type=jnp.float32, precision=HI)
-        upper[k] = panel
+        pause(k, 0)
+        upper[k] = jnp.dot(inverse, aug[k], preferred_element_type=jnp.float32, precision=HI)
 
         def update(i, _):
             there = pl.ds(pl.multiple_of(i * NB, NB), NB)
-            aug[i] -= lax.dot_general(aug[k, :, there], upper[k], (((0,), (0,)), ((), ())),
-                                      preferred_element_type=jnp.float32, precision=HI)
+            aug[i] -= lax.dot_general(
+                aug[k, :, there], upper[k], (((0,), (0,)), ((), ())), preferred_element_type=jnp.float32, precision=HI
+            )
             return 0
-        lax.fori_loop(k + 1, nblk, update, 0)
+
+        lax.fori_loop(k + 1, count, update, 0)
+        pause(k, 1)
         return 0
-    lax.fori_loop(0, nblk, eliminate, 0)
-    for k in range(nblk - 1, -1, -1):
+
+    lax.fori_loop(0, count, eliminate, 0)
+    for k in range(count - 1, -1, -1):
         x = upper[k, :, width:]
-        if k < nblk - 1:
-            x = x - jnp.dot(upper[k, :, (k + 1) * NB : width], sol[(k + 1) * NB :, :],
-                            preferred_element_type=jnp.float32, precision=HI)
+        if k < count - 1:
+            x = x - jnp.dot(
+                upper[k, :, (k + 1) * NB : width], sol[(k + 1) * NB :, :],
+                preferred_element_type=jnp.float32, precision=HI,
+            )
         sol[k * NB : (k + 1) * NB, :] = x
-        out_ref[k * NB : (k + 1) * NB, :] = x.astype(jnp.bfloat16)
-
-def solve(matrix, targets):
-    k, d = targets.shape
-    nblk = k // NB
-    return pl.pallas_call(
-        functools.partial(solve_kernel, nblk),
-        out_shape=jax.ShapeDtypeStruct((k, d), jnp.bfloat16),
-        in_specs=[pl.BlockSpec(memory_space=pltpu.VMEM)] * 2,
-        out_specs=pl.BlockSpec(memory_space=pltpu.VMEM),
-        scratch_shapes=[pltpu.VMEM((nblk, NB, k + d), jnp.float32), pltpu.VMEM((nblk, NB, k + d), jnp.float32),
-                        pltpu.VMEM((k, d), jnp.float32)],
-        compiler_params=pltpu.CompilerParams(vmem_limit_bytes=40 << 20),
-    )(matrix, targets)
+        out[k * NB : (k + 1) * NB, :] = x.astype(jnp.bfloat16)
 
 
 def remote(src, dst, sems, n, device):
@@ -123,7 +128,22 @@
         self.p, self.r = lax.axis_index(pair), lax.axis_index(ring)
         self.k = lax.axis_index("core")
         self.n = lax.axis_size(ring)
-        self.sent, self.number = [], {}
+        self.sends = self.plan()
+        self.number = {what[0]: n for n, what in enumerate(self.sends)}
+
+    def plan(self):
+        half, sends = self.n // 2, []
+        for other in (False, True):
+            if not other:
+                sends.append((("pair",), False, 0, True))
+            for way in (1, -1):
+                last = half if (way == 1) != other else half - 1
+                for s in range(1, last + 1):
+                    sends.append(((way, other, s), other, -way * (s - 1), not other and s == 1))
+            if self.core:
+                for offset in range(self.n):
+                    sends.append((("core", other, offset), other, offset, not other and offset == 0))
+        return sends
 
     @staticmethod
     def count(n, core):
@@ -143,12 +163,10 @@
 
     def copy(self, name, other, offset, own=False):
         block = self.at(other, offset)
-        n = self.number.setdefault(name, len(self.number))
-        return remote(self.source if own else block, block, self.sems, n, self.device(name))
+        return remote(self.source if own else block, block, self.sems, self.number[name], self.device(name))
 
     def send(self, *what):
         self.copy(*what).start()
-        self.sent.append(what)
 
     def arrived(self, name, dst):
         remote(dst, dst, self.sems, self.number[name], self.device(name)).wait_recv()
@@ -186,7 +204,7 @@
             for other in (False, True):
                 for offset in range(self.n):
                     self.arrived(("core", other, offset), self.at(other, offset, True))
-        for what in self.sent:
+        for what in self.sends:
             self.copy(*what).wait_send()
 
     def stages(self):
@@ -320,12 +338,14 @@
             device_id={"x_lo": peer[0], "y": peer[1]}, device_id_type=MESH,
         )
 
-    def run(self):
+    def begin(self):
         here = row_slot(self.x, self.y, 0)
         for p in range(self.bands):
             @pl.when(jnp.logical_not(self.home(p)))
             def _():
                 self.inward(p, here).start()
+
+    def sum_home(self):
         for p in range(self.bands):
             @pl.when(self.home(p))
             def _():
@@ -337,6 +357,8 @@
                 self.total[:, p * NB : (p + 1) * NB] = total
                 for number, peer in enumerate(self.peers()):
                     self.outward(p, number, peer).start()
+
+    def arrive(self):
         for p in range(self.bands):
             @pl.when(jnp.logical_not(self.home(p)))
             def _():
@@ -355,48 +377,83 @@
                     self.outward(p, number, peer).wait_send()
 
 
-def reduce_kernel(band_ref, partial_ref, matrix_ref, rows_ref, band_in, total, ring_in, last_in, *sems):
+def partial_rows(scaled, basis, partial, chunk):
+    n, height, width = partial.shape
+    calls = []
+    for i in range(0, n, chunk):
+        def call(i=i):
+            value = lax.dot_general(
+                scaled[i * height : (i + chunk) * height, :], basis[...], (((1,), (1,)), ((), ())),
+                preferred_element_type=jnp.float32,
+            )
+            partial[i : i + chunk] = value.reshape(chunk, height, width)
+        calls.append(call)
+    return calls
+
+
+def main_kernel(band_ref, scaled_ref, basis_ref, target_ref, solved_ref, rows_ref, band_in, total, partial, matrix,
+                ring_in, last_in, aug, upper, sol, *sems):
     pairs = [(sems[2 * i], sems[2 * i + 1]) for i in range(len(sems) // 2)]
     band = BandSum(band_ref, band_in, total, pairs[0], pairs[1])
-    rows = RowSum(partial_ref, ring_in, last_in, rows_ref, pairs[2], pairs[3], 2)
-    spread = Gather(total, matrix_ref, pairs[4], "x_hi", "z", True, col_slot)
+    rows = RowSum(partial, ring_in, last_in, rows_ref, pairs[2], pairs[3], 2)
+    spread = Gather(total, matrix, pairs[4], "x_hi", "z", True, col_slot)
     halves = Gather(rows_ref.at[row_slot(rows.x, rows.y, 0)], rows_ref, pairs[5], "x_lo", "y", False, row_slot)
     greet([{"x_lo": x, "y": y} for x, y in band.peers()] + col_neighbours())
-    band.run()
-    matrix_ref[col_here()] = total[...]
-    first, second = spread.stages(), rows.stages() + halves.stages()
-    for i in range(max(len(first), len(second))):
-        if i < len(first):
-            first[i]()
-        if i < len(second):
-            second[i]()
+    products = partial_rows(scaled_ref, basis_ref, partial, 4)
+    band.begin()
+    products[0]()
+    products[1]()
+    band.sum_home()
+    products[2]()
+    products[3]()
+    band.arrive()
+    first, rest = spread.stages(), rows.stages() + halves.stages()
+    first.pop(0)()
+    rest.pop(0)()
+    matrix[col_here()] = total[...]
+    for i, stage in enumerate(first):
+        stage()
+        if i in (1, 3):
+            rest.pop(0)()
+    count = solved_ref.shape[0] // NB
+    load_system(count, matrix.reshape(count * NB, count * NB), target_ref, aug)
+    beside = [[stage] for stage in rest[: 2 * count]]
+    solve_system(count, solved_ref, aug, upper, sol, beside)
+    for stage in rest[2 * count :]:
+        stage()
     band.finish()
 
 
-def reduce_rows(band, partial):
-    n, height, width = partial.shape
-    ny, nz = lax.axis_size("y"), lax.axis_size("z")
-    bands = band.shape[1] // NB
+def update_factors(band, scaled, basis, targets):
+    n, ny, nz = lax.axis_size(ROW), lax.axis_size("y"), lax.axis_size("z")
+    count, width = targets.shape
+    height = count // n
+    bands, blocks = band.shape[1] // NB, count // NB
     return pl.pallas_call(
-        reduce_kernel,
+        main_kernel,
         out_shape=[
-            jax.ShapeDtypeStruct((lax.axis_size(COL), *band.shape), jnp.float32),
-            jax.ShapeDtypeStruct(partial.shape, jnp.bfloat16),
+            jax.ShapeDtypeStruct(targets.shape, jnp.bfloat16),
+            jax.ShapeDtypeStruct((n, height, basis.shape[0]), jnp.bfloat16),
         ],
-        in_specs=[pl.BlockSpec(memory_space=pltpu.VMEM)] * 2,
+        in_specs=[pl.BlockSpec(memory_space=pltpu.VMEM)] * 4,
         out_specs=[pl.BlockSpec(memory_space=pltpu.VMEM)] * 2,
         scratch_shapes=[
             pltpu.VMEM((n, band.shape[0], NB), jnp.float32),
             pltpu.VMEM(band.shape, jnp.float32),
-            pltpu.VMEM((2, ny - 1, height, width), jnp.float32),
-            pltpu.VMEM((height, width), jnp.float32),
+            pltpu.VMEM((n, height, basis.shape[0]), jnp.float32),
+            pltpu.VMEM((lax.axis_size(COL), *band.shape), jnp.float32),
+            pltpu.VMEM((2, ny - 1, height, basis.shape[0]), jnp.float32),
+            pltpu.VMEM((height, basis.shape[0]), jnp.float32),
+            pltpu.VMEM((blocks, NB, count + width), jnp.float32),
+            pltpu.VMEM((blocks, NB, count + width), jnp.float32),
+            pltpu.VMEM(targets.shape, jnp.float32),
             pltpu.SemaphoreType.DMA((bands,)), pltpu.SemaphoreType.DMA((n,)),
             pltpu.SemaphoreType.DMA((n - 1,)), pltpu.SemaphoreType.DMA((bands,)),
             *dma_pair(4 * (ny - 1)), *dma_pair(1),
             *dma_pair(Gather.count(nz, True)), *dma_pair(Gather.count(ny, False)),
         ],
-        compiler_params=pltpu.CompilerParams(collective_id=1, has_side_effects=True, vmem_limit_bytes=48 << 20),
-    )(band, partial)
+        compiler_params=pltpu.CompilerParams(collective_id=1, has_side_effects=True, vmem_limit_bytes=56 << 20),
+    )(band, scaled, basis, targets)
 
 
 def picked(positions, size):
@@ -434,10 +491,7 @@
     first = lax.axis_index(COL) * KDEV
     band = exact_rows(lax.dynamic_slice_in_dim(scaled, first, KDEV), basis, ((1,), (1,)))
     band += exact_rows(lax.dynamic_slice_in_dim(basis, first, KDEV), scaled, ((1,), (1,)))
-    partial = exact_rows(scaled, eigenbasis, ((1,), (1,)))
-    row_count = lax.axis_size(ROW)
-    matrix, rows = reduce_rows(0.5 * band, partial.reshape(row_count, -1, partial.shape[1]))
-    solved_half = solve(matrix.reshape(removed_count, removed_count), targets)
+    solved_half, rows = update_factors(0.5 * band, scaled, eigenbasis, targets)
     change = exact_rows(solved_half, rows.reshape(removed_count, -1), ((0,), (0,)))
     return (weight.astype(jnp.float32) - change).astype(jnp.bfloat16)
 

time: 206 us -> 183 us (0.89)
  Pallas kernels: 176 us -> 160 us
  local copies, waits for them, and re-layouts: 8.24 us -> 4.29 us
  matrix products: 17.4 us -> 14.7 us
    pallas_call x2 -> x1, Pallas kernels: 133 us -> 117 us  [update_factors(): pl.pallas_call(main_kernel, out_shape=[jax.ShapeDtypeStruct(targets.shape...]
    dot_general x7 -> x6, matrix products: 17.4 us -> 14.7 us  [exact_rows(): lax.dot_general(choice, array, (dims, ((), ())), preferred_element_type=j...]
    unnamed x10 -> x6, local copies, waits for them, and re-layouts: 2.65 us -> 0.01 us
    reshape x1, local copies, waits for them, and re-layouts: 3.28 us -> 0.73 us  [shards(): columns.reshape(-1, weight.shape[0])]
    gather x1, local copies, waits for them, and re-layouts: 0.66 us -> 3.09 us  [payload_of(): basis_rows = jnp.take(eigenbasis, local_picks, axis=0)]
where the time goes in v4:
time: 183 us; the launch traced here: 182 us
  Pallas kernels  160 us (87%)
  matrix products  14.7 us (8%)
  local copies, waits for them, and re-layouts  4.29 us (2%)
  other arithmetic  3.06 us (2%)
    pallas_call x1, Pallas kernels, update_factors(): pl.pallas_call(main_kernel, out_shape=[jax.ShapeDtypeStruct(targets.shape...  117 us
    pallas_call x1, Pallas kernels, gather_col(): pl.pallas_call(gather_col_kernel, out_shape=jax.ShapeDtypeStruct((lax.axi...  43.4 us
    dot_general x6, matrix products, exact_rows(): lax.dot_general(choice, array, (dims, ((), ())), preferred_element_type=j...  14.7 us

profile of v4, /device:TPU:2, one launch (start us, length us, event | category | flops | bytes accessed | tf_op | source)
XLA Modules:
  0.0 182.3 jit_solution(13753459260452336915)
XLA Ops:
  0.0 0.8 select_reduce_fusion.1
  0.8 0.7 add.53
  1.4 0.1 convert_reduce_fusion
  1.5 0.1 select_reduce_fusion
  1.6 0.7 fusion.12
  2.3 3.1 %gather_fusion = bf16[36,1792]{1,0:T(8,128)(2,1)S(1)} fusion(bf16[896,1792]{1,0:T(8,128)(2,1)} %basis_ref.1, s32[1024]{0:T(1024)S(1)} %pad_clamp_fusion), kind=kCustom, calls=%fused_computation | custom fusion | bytes 258192 | tf_op jit(solution)/shard_map/jit(_take)/gather | solution.py:469
  5.4 0.7 compare_and_fusion
  6.1 0.1 broadcast_select_fusion
  6.1 1.6 convolution_convert_fusion
  7.8 0.0 copy-start.2
  7.8 43.4 %shard_map.55 = bf16[32,48,1792]{2,1,0:T(8,128)(2,1)S(1)} custom-call(bf16[48,1792]{1,0:T(8,128)(2,1)S(1)} %fusion.7.block_ref), custom_call_target="tpu_custom_call" | custom-call | tf_op jit(solution)/shard_map/pallas_call | solution.py:251
  51.2 0.0 copy-done.2
  51.2 5.1 %divide_convert_fusion = (bf16[768,1792]{1,0:T(8,128)(2,1)S(1)}, bf16[768,1792]{1,0:T(8,128)(2,1)S(1)}) fusion(f32[1792]{0:T(1024)S(1)} %copy-done.2, bf16[1536,1792]{1,0:T(8,128)(2,1)S(1)} %bitcast.15, s32[768]{0:T(1024)S(1)} %get-tuple-element.12), kind=kOutput, calls=%fused_computation.1 | convolution fusion | flops 4233166848 | bytes 11020288 | tf_op jit(solution)/shard_map/dot_general | solution.py:464
  56.4 0.0 copy-start
  56.4 0.8 fusion.9
  57.2 1.5 fusion.5.band_ref
  58.7 0.0 copy-done
  58.7 0.4 slice.3
  59.2 0.7 reshape.72
  59.9 2.1 %fusion.4.target_ref = bf16[768,512]{1,0:T(8,128)(2,1)} fusion(bf16[1152,512]{1,0:T(8,128)(2,1)S(1)} %reshape.72, s32[768]{0:T(1024)S(1)} %get-tuple-element.11), kind=kOutput, calls=%fused_computation.9 | convolution fusion | flops 907247616 | bytes 1969152 | tf_op jit(solution)/shard_map/dot_general | solution.py:464
  62.0 0.0 copy-start.1
  62.0 116.7 %shard_map.56 = (bf16[768,512]{1,0:T(8,128)(2,1)}, bf16[16,48,896]{2,1,0:T(8,128)(2,1)}) custom-call(f32[24,768]{1,0:T(8,128)} %fusion.5.band_ref, bf16[768,1792]{1,0:T(8,128)(2,1)} %copy-done, bf16[896,1792]{1,0:T(8,128)(2,1)} %basis_ref.1, bf16[768,512]{1,0:T(8,128)(2,1)} %fusion.4.target_ref), custom_call_target="tpu_custom_call" | custom-call | tf_op jit(solution)/shard_map/pallas_call | solution.py:432
  178.7 0.0 copy-done.1
  178.8 3.5 %subtract_convert_fusion = bf16[512,896]{1,0:T(8,128)(2,1)} fusion(bf16[512,896]{1,0:T(8,128)(2,1)S(1)} %copy-done.1, bf16[768,512]{1,0:T(8,128)(2,1)} %get-tuple-element.7, bf16[768,896]{1,0:T(8,128)(2,1)} %bitcast.17), kind=kOutput, calls=%fused_computation.7 | convolution fusion | flops 706019328 | bytes 3997696 | tf_op jit(solution)/shard_map/dot_general | solution.py:464
  (4 shorter events, 0.1 us)
Async XLA Ops:
  7.8 43.4 %copy-start.2 = (f32[1792]{0:T(1024)S(1)}, f32[1792]{0:T(1024)}, u32[]{:S(2)}) copy-start(f32[1792]{0:T(1024)} %param.7) | copy-start | bytes 21508
  56.4 2.4 %copy-start = (bf16[768,1792]{1,0:T(8,128)(2,1)}, bf16[768,1792]{1,0:T(8,128)(2,1)S(1)}, u32[]{:S(2)}) copy-start(bf16[768,1792]{1,0:T(8,128)(2,1)S(1)} %get-tuple-element.9.scaled_ref) | copy-start | bytes 8257540
  62.0 116.7 %copy-start.1 = (bf16[512,896]{1,0:T(8,128)(2,1)S(1)}, bf16[512,896]{1,0:T(8,128)(2,1)}, u32[]{:S(2)}) copy-start(bf16[512,896]{1,0:T(8,128)(2,1)} %param.5) | copy-start | bytes 2752516

commit v5 on v4

--- a/solution.py
+++ b/solution.py
@@ -27,38 +27,64 @@
 
 
 HI = lax.Precision.HIGHEST
-NB=128
-
-def invert_block(block):
+NB = 128
+PAUSES = (4, 9)
+BREAKS = len(PAUSES) + 2
+PARTS = 3
+EARLY = (0, 0, 1, 2, 2, 2, 2, 2, 0)
+
+def lane_spread(tile, lane):
+    return jnp.broadcast_to(tile[:, lane : lane + 1], tile.shape)
+
+
+def invert_block(block, pause):
     lane = lax.broadcasted_iota(jnp.int32, (8, NB), 1)
     sub = lax.broadcasted_iota(jnp.int32, (8, NB), 0)
-    tiles = [block[8 * i : 8 * i + 8, :] for i in range(NB // 8)]
-    for b in range(NB // 8):
+    count = NB // 8
+    tiles = [block[8 * i : 8 * i + 8, :] for i in range(count)]
+    for b in range(count):
         here = (lane >= 8 * b) & (lane < 8 * b + 8)
-        columns = [[jnp.broadcast_to(t[:, 8 * b + j : 8 * b + j + 1], (8, NB)) for j in range(8)] for t in tiles]
-        pivots = list(columns[b])
+        pivots = [lane_spread(tiles[b], 8 * b + j) for j in range(8)]
         panel = jnp.where(here, jnp.where(lane - 8 * b == sub, 1.0, 0.0), tiles[b])
         for p in range(8):
             own = sub == p
             factor = pivots[p]
             inv = 1.0 / jnp.broadcast_to(factor[p : p + 1, :], (8, NB))
+
             def step(x):
                 scaled = jnp.broadcast_to(x[p : p + 1, :], (8, NB)) * inv
                 return jnp.where(own, scaled, x - factor * scaled)
+
             for q in range(p + 1, 8):
                 pivots[q] = step(pivots[q])
             panel = step(panel)
-        rows = [jnp.broadcast_to(panel[j : j + 1, :], (8, NB)) for j in range(8)]
-        for i in range(NB // 8):
+        if b < count - 1:
+            parts = [
+                lane_spread(tiles[b + 1], 8 * b + j) * jnp.broadcast_to(panel[j : j + 1, :], (8, NB)) for j in range(8)
+            ]
+            while len(parts) > 1:
+                parts = [parts[2 * m] + parts[2 * m + 1] for m in range(len(parts) // 2)]
+            following = jnp.where(here, 0.0, tiles[b + 1]) - parts[0]
+        spread = [panel]
+        if b:
+            spread.insert(0, jnp.zeros((8 * b, NB), jnp.float32))
+        if b < count - 1:
+            spread.append(jnp.zeros((NB - 8 * b - 8, NB), jnp.float32))
+        change = jnp.dot(
+            jnp.concatenate(tiles, axis=0), jnp.concatenate(spread, axis=0),
+            preferred_element_type=jnp.float32, precision=HI,
+        )
+        for i in range(count):
             if i == b:
                 tiles[i] = panel
+            elif i == b + 1:
+                tiles[i] = following
             else:
-                t = jnp.where(here, 0.0, tiles[i])
-                parts = [columns[i][j] * rows[j] for j in range(8)]
-                while len(parts) > 1:
-                    parts = [parts[2 * m] + parts[2 * m + 1] for m in range(len(parts) // 2)]
-                tiles[i] = t - parts[0]
+                tiles[i] = jnp.where(here, 0.0, tiles[i]) - change[8 * i : 8 * i + 8, :]
+        if b in PAUSES:
+            pause(PAUSES.index(b))
     return jnp.concatenate(tiles, axis=0)
+
 
 def load_system(count, matrix, targets, aug):
     width = count * NB
@@ -72,16 +98,17 @@
 
     def pause(k, which):
         for i in range(count):
-            if 2 * i + which < len(beside):
+            stages = beside[BREAKS * i + which]
+            if stages:
                 @pl.when(k == i)
                 def _():
-                    for call in beside[2 * i + which]:
-                        call()
+                    for stage in stages:
+                        stage()
 
     def eliminate(k, _):
         here = pl.ds(pl.multiple_of(k * NB, NB), NB)
-        inverse = invert_block(aug[k, :, here])
-        pause(k, 0)
+        inverse = invert_block(aug[k, :, here], functools.partial(pause, k))
+        pause(k, BREAKS - 2)
         upper[k] = jnp.dot(inverse, aug[k], preferred_element_type=jnp.float32, precision=HI)
 
         def update(i, _):
@@ -92,7 +119,7 @@
             return 0
 
         lax.fori_loop(k + 1, count, update, 0)
-        pause(k, 1)
+        pause(k, BREAKS - 1)
         return 0
 
     lax.fori_loop(0, count, eliminate, 0)
@@ -122,37 +149,45 @@
 
 
 class Gather:
-    def __init__(self, source, out, sems, pair, ring, core, slot):
+    def __init__(self, source, out, sems, pair, ring, core, slot, near=0, cuts=None):
         self.source, self.out, self.sems = source, out, sems
         self.pair, self.ring, self.core, self.slot = pair, ring, core, slot
+        self.near = near
+        self.cuts = cuts or [pl.ds(0, source.shape[0])]
         self.p, self.r = lax.axis_index(pair), lax.axis_index(ring)
         self.k = lax.axis_index("core")
         self.n = lax.axis_size(ring)
         self.sends = self.plan()
         self.number = {what[0]: n for n, what in enumerate(self.sends)}
 
+    def last(self, other, way):
+        return self.n // 2 if (way == 1) != other else self.n // 2 - 1
+
     def plan(self):
-        half, sends = self.n // 2, []
-        for other in (False, True):
-            if not other:
-                sends.append((("pair",), False, 0, True))
+        sends = []
+        for u in range(len(self.cuts)):
+            sends.append((("pair", u, 1, 0), False, 0, True))
             for way in (1, -1):
-                last = half if (way == 1) != other else half - 1
-                for s in range(1, last + 1):
-                    sends.append(((way, other, s), other, -way * (s - 1), not other and s == 1))
+                for s in range(1, self.near + 1):
+                    sends.append((("pair", u, way, s), False, -way * s, False))
+                for s in range(1, self.last(False, way) + 1):
+                    sends.append(((way, u, False, s), False, -way * (s - 1), s == 1))
+                for s in range(self.near + 1, self.last(True, way) + 1):
+                    sends.append(((way, u, True, s), True, -way * (s - 1), False))
             if self.core:
-                for offset in range(self.n):
-                    sends.append((("core", other, offset), other, offset, not other and offset == 0))
+                for other in (False, True):
+                    for offset in range(self.n):
+                        sends.append((("core", u, other, offset), other, offset, not other and offset == 0))
         return sends
 
     @staticmethod
-    def count(n, core):
-        return 1 + 2 * (n - 1) + (2 * n if core else 0)
-
-    def at(self, other, offset, sibling=False):
+    def count(n, core, near=0, parts=1):
+        return parts * (1 + 2 * near + (n - 1) + (n - 1 - 2 * near) + (2 * n if core else 0))
+
+    def at(self, u, other, offset, sibling=False):
         p = 1 - self.p if other else self.p
         k = 1 - self.k if sibling else self.k
-        return self.out.at[self.slot(p, lax.rem(self.r + offset + self.n, self.n), k)]
+        return self.out.at[self.slot(p, lax.rem(self.r + offset + self.n, self.n), k), self.cuts[u]]
 
     def device(self, name):
         if name[0] == "pair":
@@ -161,55 +196,67 @@
             return {"core": 1 - self.k}
         return {self.ring: lax.rem(self.r + name[0] + self.n, self.n)}
 
-    def copy(self, name, other, offset, own=False):
-        block = self.at(other, offset)
-        return remote(self.source if own else block, block, self.sems, self.number[name], self.device(name))
-
-    def send(self, *what):
-        self.copy(*what).start()
-
-    def arrived(self, name, dst):
+    def copy(self, name):
+        n = self.number[name]
+        _, other, offset, own = self.sends[n]
+        block = self.at(name[1], other, offset)
+        return remote(self.source.at[self.cuts[name[1]]] if own else block, block, self.sems, n, self.device(name))
+
+    def send(self, *name):
+        self.copy(name).start()
+
+    def arrived(self, dst, *name):
         remote(dst, dst, self.sems, self.number[name], self.device(name)).wait_recv()
 
-    def share(self, other, offset, own=False):
+    def share(self, u, other, offset):
         if self.core:
-            self.send(("core", other, offset % self.n), other, offset, own)
-
-    def begin(self):
-        self.send(("pair",), False, 0, True)
+            self.send("core", u, other, offset % self.n)
+
+    def begin(self, u):
+        self.send("pair", u, 1, 0)
         for way in (1, -1):
-            self.send((way, False, 1), False, 0, True)
-        self.share(False, 0, True)
-
-    def spread_pair(self):
-        self.arrived(("pair",), self.at(True, 0))
+            self.send(way, u, False, 1)
+        self.share(u, False, 0)
+
+    def cross(self, s, u):
+        for way in (1, -1) if s else (1,):
+            self.arrived(self.at(u, True, -way * s), "pair", u, way, s)
+            for onward in (way,) if s else (1, -1):
+                if s == self.near and s < self.last(True, onward):
+                    self.send(onward, u, True, s + 1)
+            self.share(u, True, -way * s)
+
+    def advance(self, other, s, u):
         for way in (1, -1):
-            self.send((way, True, 1), True, 0)
-        self.share(True, 0)
-
-    def advance(self, s):
-        half = self.n // 2
-        for other in (False, True):
-            for way in (1, -1):
-                last = half if (way == 1) != other else half - 1
-                if s > last:
-                    continue
-                self.arrived((way, other, s), self.at(other, -way * s))
-                if s < last:
-                    self.send((way, other, s + 1), other, -way * s)
-                self.share(other, -way * s)
+            if s > self.last(other, way):
+                continue
+            self.arrived(self.at(u, other, -way * s), way, u, other, s)
+            if s < self.last(other, way):
+                self.send(way, u, other, s + 1)
+            if not other and s <= self.near:
+                self.send("pair", u, way, s)
+            self.share(u, other, -way * s)
 
     def finish(self):
-        if self.core:
-            for other in (False, True):
-                for offset in range(self.n):
-                    self.arrived(("core", other, offset), self.at(other, offset, True))
+        for u in range(len(self.cuts)):
+            if self.core:
+                for other in (False, True):
+                    for offset in range(self.n):
+                        self.arrived(self.at(u, other, offset, True), "core", u, other, offset)
         for what in self.sends:
-            self.copy(*what).wait_send()
+            self.copy(what[0]).wait_send()
 
     def stages(self):
-        rest = [functools.partial(self.advance, s) for s in range(1, self.n // 2 + 1)]
-        return [self.begin, self.spread_pair, *rest, self.finish]
+        own = [functools.partial(self.advance, False, s) for s in range(1, self.n // 2 + 1)]
+        pair = [functools.partial(self.cross, s) for s in range(self.near + 1)]
+        pair += [functools.partial(self.advance, True, s) for s in range(self.near + 1, self.n // 2 + 1)]
+        mixed = [stage for both in zip(own, pair) for stage in both] + pair[len(own):]
+
+        def each(stage):
+            for u in range(len(self.cuts)):
+                stage(u)
+
+        return [functools.partial(each, stage) for stage in [self.begin, *mixed]] + [self.finish]
 
 
 def col_slot(p, r, k):
@@ -234,6 +281,11 @@
     return col_slot(lax.axis_index("x_hi"), lax.axis_index("z"), lax.axis_index("core"))
 
 
+def row_cuts(ref, parts):
+    rows = ref.shape[0] // parts
+    return [pl.ds(u * rows, rows) for u in range(parts)]
+
+
 def dma_pair(*shape):
     return [pltpu.SemaphoreType.DMA(shape), pltpu.SemaphoreType.DMA(shape)]
 
@@ -242,7 +294,8 @@
     mine = pltpu.make_async_copy(block_ref, out_ref.at[col_here()], local)
     mine.start()
     greet(col_neighbours())
-    for stage in Gather(block_ref, out_ref, (send, recv), "x_hi", "z", True, col_slot).stages():
+    gather = Gather(block_ref, out_ref, (send, recv), "x_hi", "z", True, col_slot, 1, row_cuts(block_ref, PARTS))
+    for stage in gather.stages():
         stage()
     mine.wait()
 
@@ -253,7 +306,7 @@
         out_shape=jax.ShapeDtypeStruct((lax.axis_size(COL), *block.shape), block.dtype),
         in_specs=[pl.BlockSpec(memory_space=pltpu.VMEM)],
         out_specs=pl.BlockSpec(memory_space=pltpu.VMEM),
-        scratch_shapes=[*dma_pair(Gather.count(lax.axis_size("z"), True)), pltpu.SemaphoreType.DMA],
+        scratch_shapes=[*dma_pair(Gather.count(lax.axis_size("z"), True, 1, PARTS)), pltpu.SemaphoreType.DMA],
         compiler_params=pltpu.CompilerParams(collective_id=0, has_side_effects=True, vmem_limit_bytes=40 << 20),
     )(block)
 
@@ -283,29 +336,34 @@
         for w, u in self.every():
             self.copy(w, u, 0).start()
 
-    def advance(self, s):
-        for w, u in self.every():
+    def advance(self, s, u):
+        for w in range(2):
             self.copy(w, u, s).wait_recv()
             self.ring_in[w, s, self.cuts[u]] += self.term(w, 2 + s, u)[...]
             if s < self.n - 2:
                 self.copy(w, u, s + 1).start()
 
-    def last(self):
-        return remote(self.ring_in.at[1 - self.x, self.n - 2], self.last_in, self.last_sems, 0, {"x_lo": 1 - self.x})
-
-    def cross(self):
-        self.last().start()
+    def last(self, u):
+        src = self.ring_in.at[1 - self.x, self.n - 2, self.cuts[u]]
+        return remote(src, self.last_in.at[self.cuts[u]], self.last_sems, u, {"x_lo": 1 - self.x})
+
+    def cross(self, u):
+        self.last(u).start()
+
+    def round(self, u):
+        self.last(u).wait_recv()
+        value = self.ring_in[self.x, self.n - 2, self.cuts[u]] + self.last_in[self.cuts[u]]
+        self.done[row_slot(self.x, self.y, 0), self.cuts[u]] = value.astype(jnp.bfloat16)
 
     def finish(self):
-        self.last().wait_recv()
-        self.done[row_slot(self.x, self.y, 0)] = (self.ring_in[self.x, self.n - 2] + self.last_in[...]).astype(jnp.bfloat16)
         for w, u in self.every():
             for s in range(self.n - 1):
                 self.copy(w, u, s).wait_send()
-        self.last().wait_send()
-
-    def stages(self):
-        return [self.begin, *[functools.partial(self.advance, s) for s in range(self.n - 1)], self.cross, self.finish]
+        for u in range(len(self.cuts)):
+            self.last(u).wait_send()
+
+    def steps(self):
+        return [functools.partial(self.advance, s, u) for s in range(self.n - 1) for u in range(len(self.cuts))]
 
 
 class BandSum:
@@ -395,32 +453,42 @@
                 ring_in, last_in, aug, upper, sol, *sems):
     pairs = [(sems[2 * i], sems[2 * i + 1]) for i in range(len(sems) // 2)]
     band = BandSum(band_ref, band_in, total, pairs[0], pairs[1])
-    rows = RowSum(partial, ring_in, last_in, rows_ref, pairs[2], pairs[3], 2)
-    spread = Gather(total, matrix, pairs[4], "x_hi", "z", True, col_slot)
-    halves = Gather(rows_ref.at[row_slot(rows.x, rows.y, 0)], rows_ref, pairs[5], "x_lo", "y", False, row_slot)
+    rows = RowSum(partial, ring_in, last_in, rows_ref, pairs[2], pairs[3], PARTS)
+    spread = Gather(total, matrix, pairs[4], "x_hi", "z", True, col_slot, 1, row_cuts(total, PARTS))
+    own_rows = rows_ref.at[row_slot(rows.x, rows.y, 0)]
+    halves = Gather(own_rows, rows_ref, pairs[5], "x_lo", "y", False, row_slot, 1, row_cuts(own_rows, PARTS))
     greet([{"x_lo": x, "y": y} for x, y in band.peers()] + col_neighbours())
     products = partial_rows(scaled_ref, basis_ref, partial, 4)
     band.begin()
+    band.sum_home()
+    band.arrive()
+    first, rest = spread.stages(), rows.steps()
+    for u in range(PARTS):
+        rest.insert(len(rest) - PARTS + 1 + u, functools.partial(rows.cross, u))
+    for u in range(PARTS):
+        rest += [functools.partial(rows.round, u), functools.partial(halves.begin, u)]
+    rest += halves.stages()[1:-1]
+    first.pop(0)()
+    matrix[col_here()] = total[...]
     products[0]()
     products[1]()
-    band.sum_home()
+    first.pop(0)()
     products[2]()
     products[3]()
-    band.arrive()
-    first, rest = spread.stages(), rows.stages() + halves.stages()
-    first.pop(0)()
-    rest.pop(0)()
-    matrix[col_here()] = total[...]
-    for i, stage in enumerate(first):
+    rows.begin()
+    for early, stage in zip(EARLY, first, strict=True):
         stage()
-        if i in (1, 3):
+        for _ in range(early):
             rest.pop(0)()
     count = solved_ref.shape[0] // NB
     load_system(count, matrix.reshape(count * NB, count * NB), target_ref, aug)
-    beside = [[stage] for stage in rest[: 2 * count]]
+    breaks = BREAKS * count
+    beside = [[] for _ in range(breaks)]
+    for i, stage in enumerate(rest):
+        beside[i * breaks // len(rest)].append(stage)
     solve_system(count, solved_ref, aug, upper, sol, beside)
-    for stage in rest[2 * count :]:
-        stage()
+    halves.finish()
+    rows.finish()
     band.finish()
 
 
@@ -449,8 +517,8 @@
             pltpu.VMEM(targets.shape, jnp.float32),
             pltpu.SemaphoreType.DMA((bands,)), pltpu.SemaphoreType.DMA((n,)),
             pltpu.SemaphoreType.DMA((n - 1,)), pltpu.SemaphoreType.DMA((bands,)),
-            *dma_pair(4 * (ny - 1)), *dma_pair(1),
-            *dma_pair(Gather.count(nz, True)), *dma_pair(Gather.count(ny, False)),
+            *dma_pair(2 * PARTS * (ny - 1)), *dma_pair(PARTS),
+            *dma_pair(Gather.count(nz, True, 1, PARTS)), *dma_pair(Gather.count(ny, False, 1, PARTS)),
         ],
         compiler_params=pltpu.CompilerParams(collective_id=1, has_side_effects=True, vmem_limit_bytes=56 << 20),
     )(band, scaled, basis, targets)

time: 183 us -> 169 us (0.923)
  Pallas kernels: 160 us -> 147 us
    pallas_call x1, Pallas kernels: 117 us -> 107 us  [update_factors(): pl.pallas_call(main_kernel, out_shape=[jax.ShapeDtypeStruct(targets.shape...]
    pallas_call x1, Pallas kernels: 43.4 us -> 40.1 us  [gather_col(): pl.pallas_call(gather_col_kernel, out_shape=jax.ShapeDtypeStruct((lax.axi...]
where the time goes in v5:
time: 169 us
  Pallas kernels  147 us (87%)
  matrix products  14.7 us (9%)
  local copies, waits for them, and re-layouts  4.29 us (3%)
  other arithmetic  3.06 us (2%)
    pallas_call x1, Pallas kernels, update_factors(): pl.pallas_call(main_kernel, out_shape=[jax.ShapeDtypeStruct(targets.shape...  107 us
    pallas_call x1, Pallas kernels, gather_col(): pl.pallas_call(gather_col_kernel, out_shape=jax.ShapeDtypeStruct((lax.axi...  40.1 us
    dot_general x6, matrix products, exact_rows(): lax.dot_general(choice, array, (dims, ((), ())), preferred_element_type=j...  14.7 us

profile of v5, /device:TPU:2, one launch (start us, length us, event | category | flops | bytes accessed | tf_op | source)
XLA Modules:
  0.0 169.0 jit_solution(4290439554549739451)
XLA Ops:
  0.0 0.8 select_reduce_fusion.1
  0.8 0.7 add.53
  1.4 0.1 convert_reduce_fusion
  1.5 0.1 select_reduce_fusion
  1.6 0.7 fusion.12
  2.3 3.1 %gather_fusion = bf16[36,1792]{1,0:T(8,128)(2,1)S(1)} fusion(bf16[896,1792]{1,0:T(8,128)(2,1)} %basis_ref.1, s32[1024]{0:T(1024)S(1)} %pad_clamp_fusion), kind=kCustom, calls=%fused_computation | custom fusion | bytes 258192 | tf_op jit(solution)/shard_map/jit(_take)/gather | solution.py:537
  5.4 0.7 compare_and_fusion
  6.1 0.1 broadcast_select_fusion
  6.1 1.6 convolution_convert_fusion
  7.8 0.0 copy-start.2
  7.8 40.1 %shard_map.55 = bf16[32,48,1792]{2,1,0:T(8,128)(2,1)S(1)} custom-call(bf16[48,1792]{1,0:T(8,128)(2,1)S(1)} %fusion.7.block_ref), custom_call_target="tpu_custom_call" | custom-call | tf_op jit(solution)/shard_map/pallas_call | solution.py:304
  47.9 0.0 copy-done.2
  47.9 5.1 %divide_convert_fusion = (bf16[768,1792]{1,0:T(8,128)(2,1)S(1)}, bf16[768,1792]{1,0:T(8,128)(2,1)S(1)}) fusion(f32[1792]{0:T(1024)S(1)} %copy-done.2, bf16[1536,1792]{1,0:T(8,128)(2,1)S(1)} %bitcast.15, s32[768]{0:T(1024)S(1)} %get-tuple-element.12), kind=kOutput, calls=%fused_computation.1 | convolution fusion | flops 4233166848 | bytes 11020288 | tf_op jit(solution)/shard_map/dot_general | solution.py:532
  53.1 0.0 copy-start
  53.1 0.8 fusion.9
  53.9 1.5 fusion.5.band_ref
  55.5 0.0 copy-done
  55.5 0.4 slice.3
  55.9 0.7 reshape.72
  56.6 2.1 %fusion.4.target_ref = bf16[768,512]{1,0:T(8,128)(2,1)} fusion(bf16[1152,512]{1,0:T(8,128)(2,1)S(1)} %reshape.72, s32[768]{0:T(1024)S(1)} %get-tuple-element.11), kind=kOutput, calls=%fused_computation.9 | convolution fusion | flops 907247616 | bytes 1969152 | tf_op jit(solution)/shard_map/dot_general | solution.py:532
  58.7 0.0 copy-start.1
  58.7 106.8 %shard_map.56 = (bf16[768,512]{1,0:T(8,128)(2,1)}, bf16[16,48,896]{2,1,0:T(8,128)(2,1)}) custom-call(f32[24,768]{1,0:T(8,128)} %fusion.5.band_ref, bf16[768,1792]{1,0:T(8,128)(2,1)} %copy-done, bf16[896,1792]{1,0:T(8,128)(2,1)} %basis_ref.1, bf16[768,512]{1,0:T(8,128)(2,1)} %fusion.4.target_ref), custom_call_target="tpu_custom_call" | custom-call | tf_op jit(solution)/shard_map/pallas_call | solution.py:500
  165.5 0.0 copy-done.1
  165.5 3.5 %subtract_convert_fusion = bf16[512,896]{1,0:T(8,128)(2,1)} fusion(bf16[512,896]{1,0:T(8,128)(2,1)S(1)} %copy-done.1, bf16[768,512]{1,0:T(8,128)(2,1)} %get-tuple-element.7, bf16[768,896]{1,0:T(8,128)(2,1)} %bitcast.17), kind=kOutput, calls=%fused_computation.7 | convolution fusion | flops 706019328 | bytes 3997696 | tf_op jit(solution)/shard_map/dot_general | solution.py:532
  (4 shorter events, 0.1 us)
Async XLA Ops:
  7.8 40.1 %copy-start.2 = (f32[1792]{0:T(1024)S(1)}, f32[1792]{0:T(1024)}, u32[]{:S(2)}) copy-start(f32[1792]{0:T(1024)} %param.7) | copy-start | bytes 21508
  53.1 2.4 %copy-start = (bf16[768,1792]{1,0:T(8,128)(2,1)}, bf16[768,1792]{1,0:T(8,128)(2,1)S(1)}, u32[]{:S(2)}) copy-start(bf16[768,1792]{1,0:T(8,128)(2,1)S(1)} %get-tuple-element.9.scaled_ref) | copy-start | bytes 8257540
  58.7 106.8 %copy-start.1 = (bf16[512,896]{1,0:T(8,128)(2,1)S(1)}, bf16[512,896]{1,0:T(8,128)(2,1)}, u32[]{:S(2)}) copy-start(bf16[512,896]{1,0:T(8,128)(2,1)} %param.5) | copy-start | bytes 2752516

commit v6 on v5

--- a/solution.py
+++ b/solution.py
@@ -28,7 +28,7 @@
 
 HI = lax.Precision.HIGHEST
 NB = 128
-PAUSES = (4, 9)
+PAUSES = (2, 5, 8, 11)
 BREAKS = len(PAUSES) + 2
 PARTS = 3
 EARLY = (0, 0, 1, 2, 2, 2, 2, 2, 0)

time: 169 us -> 172 us (1.018)
  Pallas kernels: 147 us -> 150 us
    pallas_call x1, Pallas kernels: 107 us -> 110 us  [update_factors(): pl.pallas_call(main_kernel, out_shape=[jax.ShapeDtypeStruct(targets.shape...]
where the time goes in v6:
time: 172 us
  Pallas kernels  150 us (87%)
  matrix products  14.7 us (9%)
  local copies, waits for them, and re-layouts  4.29 us (2%)
  other arithmetic  3.06 us (2%)
    pallas_call x1, Pallas kernels, update_factors(): pl.pallas_call(main_kernel, out_shape=[jax.ShapeDtypeStruct(targets.shape...  110 us
    pallas_call x1, Pallas kernels, gather_col(): pl.pallas_call(gather_col_kernel, out_shape=jax.ShapeDtypeStruct((lax.axi...  40.1 us
    dot_general x6, matrix products, exact_rows(): lax.dot_general(choice, array, (dims, ((), ())), preferred_element_type=j...  14.7 us

profile of v6, /device:TPU:2, one launch (start us, length us, event | category | flops | bytes accessed | tf_op | source)
XLA Modules:
  0.0 172.0 jit_solution(14163244006774337562)
XLA Ops:
  0.0 0.8 select_reduce_fusion.1
  0.8 0.7 add.53
  1.4 0.1 convert_reduce_fusion
  1.5 0.1 select_reduce_fusion
  1.6 0.7 fusion.12
  2.3 3.1 %gather_fusion = bf16[36,1792]{1,0:T(8,128)(2,1)S(1)} fusion(bf16[896,1792]{1,0:T(8,128)(2,1)} %basis_ref.1, s32[1024]{0:T(1024)S(1)} %pad_clamp_fusion), kind=kCustom, calls=%fused_computation | custom fusion | bytes 258192 | tf_op jit(solution)/shard_map/jit(_take)/gather | solution.py:537
  5.4 0.7 compare_and_fusion
  6.1 0.1 broadcast_select_fusion
  6.1 1.6 convolution_convert_fusion
  7.8 0.0 copy-start.2
  7.8 40.1 %shard_map.55 = bf16[32,48,1792]{2,1,0:T(8,128)(2,1)S(1)} custom-call(bf16[48,1792]{1,0:T(8,128)(2,1)S(1)} %fusion.7.block_ref), custom_call_target="tpu_custom_call" | custom-call | tf_op jit(solution)/shard_map/pallas_call | solution.py:304
  47.9 0.0 copy-done.2
  47.9 5.1 %divide_convert_fusion = (bf16[768,1792]{1,0:T(8,128)(2,1)S(1)}, bf16[768,1792]{1,0:T(8,128)(2,1)S(1)}) fusion(f32[1792]{0:T(1024)S(1)} %copy-done.2, bf16[1536,1792]{1,0:T(8,128)(2,1)S(1)} %bitcast.15, s32[768]{0:T(1024)S(1)} %get-tuple-element.12), kind=kOutput, calls=%fused_computation.1 | convolution fusion | flops 4233166848 | bytes 11020288 | tf_op jit(solution)/shard_map/dot_general | solution.py:532
  53.1 0.0 copy-start
  53.1 0.8 fusion.9
  53.9 1.5 fusion.5.band_ref
  55.5 0.0 copy-done
  55.5 0.4 slice.3
  55.9 0.7 reshape.72
  56.6 2.1 %fusion.4.target_ref = bf16[768,512]{1,0:T(8,128)(2,1)} fusion(bf16[1152,512]{1,0:T(8,128)(2,1)S(1)} %reshape.72, s32[768]{0:T(1024)S(1)} %get-tuple-element.11), kind=kOutput, calls=%fused_computation.9 | convolution fusion | flops 907247616 | bytes 1969152 | tf_op jit(solution)/shard_map/dot_general | solution.py:532
  58.7 0.0 copy-start.1
  58.7 109.7 %shard_map.56 = (bf16[768,512]{1,0:T(8,128)(2,1)}, bf16[16,48,896]{2,1,0:T(8,128)(2,1)}) custom-call(f32[24,768]{1,0:T(8,128)} %fusion.5.band_ref, bf16[768,1792]{1,0:T(8,128)(2,1)} %copy-done, bf16[896,1792]{1,0:T(8,128)(2,1)} %basis_ref.1, bf16[768,512]{1,0:T(8,128)(2,1)} %fusion.4.target_ref), custom_call_target="tpu_custom_call" | custom-call | tf_op jit(solution)/shard_map/pallas_call | solution.py:500
  168.4 0.0 copy-done.1
  168.5 3.5 %subtract_convert_fusion = bf16[512,896]{1,0:T(8,128)(2,1)} fusion(bf16[512,896]{1,0:T(8,128)(2,1)S(1)} %copy-done.1, bf16[768,512]{1,0:T(8,128)(2,1)} %get-tuple-element.7, bf16[768,896]{1,0:T(8,128)(2,1)} %bitcast.17), kind=kOutput, calls=%fused_computation.7 | convolution fusion | flops 706019328 | bytes 3997696 | tf_op jit(solution)/shard_map/dot_general | solution.py:532
  (4 shorter events, 0.1 us)
Async XLA Ops:
  7.8 40.1 %copy-start.2 = (f32[1792]{0:T(1024)S(1)}, f32[1792]{0:T(1024)}, u32[]{:S(2)}) copy-start(f32[1792]{0:T(1024)} %param.7) | copy-start | bytes 21508
  53.1 2.4 %copy-start = (bf16[768,1792]{1,0:T(8,128)(2,1)}, bf16[768,1792]{1,0:T(8,128)(2,1)S(1)}, u32[]{:S(2)}) copy-start(bf16[768,1792]{1,0:T(8,128)(2,1)S(1)} %get-tuple-element.9.scaled_ref) | copy-start | bytes 8257540
  58.7 109.7 %copy-start.1 = (bf16[512,896]{1,0:T(8,128)(2,1)S(1)}, bf16[512,896]{1,0:T(8,128)(2,1)}, u32[]{:S(2)}) copy-start(bf16[512,896]{1,0:T(8,128)(2,1)} %param.5) | copy-start | bytes 2752516
